TPU v7x, 32 devices: a whole 2x2x4 slice. The times are simulated.
32 devices in a mesh: parts: 2 (over x), wide: 16 (over z, y, core).
Axes of the slice: x: 2, y: 2, z: 4, core: 2. Of those that a mesh axis runs over, the one named last changes fastest.
Arguments:
- voxels: bfloat16 [32768, 256], P(('parts', 'wide')), parts along dimension 0, may hold values from -16 to 16
- regular_window: int32 [32768], P(('parts', 'wide')), parts along dimension 0, may hold values from 0 to 127, never falling along the last dimension, each value on 1 to 256 neighbouring positions
- shifted_window: int32 [32768], P(('parts', 'wide')), parts along dimension 0, may hold values from 0 to 127, never falling along the last dimension, each value on 1 to 256 neighbouring positions
- dest: int32 [32768], P(('parts', 'wide')), parts along dimension 0, may hold values from 0 to 16383, as said below
- w_qkv: bfloat16 [2, 256, 768], replicated, may hold values from -0.375 to 0.375
- w_out: bfloat16 [2, 256, 256], replicated, may hold values from -1.5 to 1.5
- gain: float32 [2, 256], replicated, may hold values from 0.1 to 1.9
- temper: float32 [2, 8], replicated, may hold values from 0.5 to 6
Outputs:
- shifted_out: bfloat16 [32768, 256], P(('parts', 'wide')), parts along dimension 0
There are 2 independent parts, one for each index of `parts`. A program takes and returns all parts, laid end to end along the dimension named above; an argument that names none is the same for every part. Nothing has to cross between parts.
Inputs may be any that keep to these rules, and one draw needn't show every extreme that they name: `regular_window`: window ids never fall along the order; every window has 1 to 256 voxels and one has exactly 256. `shifted_window`: window ids never fall along the order; every window has 1 to 256 voxels and one has exactly 256. dest is a permutation. Counting blocks of 1024 consecutive positions, at most 128 voxels go from one block of the regular order to one block of the shifted order, and some pair reaches 128; the count from a block to the block k places further along, cyclically, is the same for every block.
All inputs are finite; a program needn't handle non-finite values.
Results may differ from a plain program's by a relative error of at most 0.007.
The roundings to bfloat16 on the way count: a program that leaves them out, or rounds other values in their place, can miss the bound.
Values may be sent and summed in bfloat16 or wider, within the bound.
No kernel may reach another device: no remote copies, remote signals or barrier semaphores. Data moves between devices by JAX's collectives and lax.ppermute only.
A program may use at most 64 MiB of HBM per device.

v0:
```python
import math

import jax
import jax.numpy as jnp
from jax import lax
from jax.sharding import PartitionSpec as P

HEADS = 8


epsilon = 1e-05
masked_score = -1e30


def extended(block, sides, width):
    for axis, dim in sides:
        count = lax.axis_size(axis)
        forward = [(i, i + 1) for i in range(count - 1)]
        backward = [(target, source) for source, target in forward]
        low = lax.ppermute(
            lax.slice_in_dim(block, block.shape[dim] - width, None, axis=dim), axis, forward
        )
        high = lax.ppermute(lax.slice_in_dim(block, 0, width, axis=dim), axis, backward)
        block = jnp.concatenate([low, block, high], axis=dim)
    return block


def settle(hidden, attended, w_out_layer, gain_layer):
    summed = hidden.astype(jnp.float32) + jnp.dot(
        attended, w_out_layer, preferred_element_type=jnp.float32
    )
    center = jnp.mean(summed, axis=1, keepdims=True)
    spread = jnp.mean(jnp.square(summed - center), axis=1, keepdims=True)
    return ((summed - center) * lax.rsqrt(spread + epsilon) * gain_layer).astype(jnp.bfloat16)


def window_attention(queries, padded, marks_own, marks_pad, factor, rim_width):
    total_rows = queries.shape[0]
    channels = queries.shape[1]
    head_dim = channels // HEADS
    block_rows = min(512, total_rows)
    key_rows = block_rows + 2 * rim_width
    results = []
    for number in range(total_rows // block_rows):
        first_row = number * block_rows
        query_block = queries[first_row : first_row + block_rows]
        key_block = padded[first_row : first_row + key_rows]
        mark_query = marks_own[first_row : first_row + block_rows]
        mark_key = marks_pad[first_row : first_row + key_rows]
        same_window = mark_query[:, None] == mark_key[None, :]

        def per_head(
            head_index, query_block=query_block, key_block=key_block, same_window=same_window
        ):
            query_part = lax.dynamic_slice_in_dim(query_block, head_index * head_dim, head_dim, 1)
            keys_part = lax.dynamic_slice_in_dim(key_block, head_index * head_dim, head_dim, 1)
            values_part = lax.dynamic_slice_in_dim(
                key_block, channels + head_index * head_dim, head_dim, 1
            )
            scores = lax.dot_general(
                query_part, keys_part, (((1,), (1,)), ((), ())), preferred_element_type=jnp.float32
            )
            scores = scores * factor[head_index]
            scores = jnp.where(same_window, scores, masked_score)
            highest = jnp.max(scores, axis=1, keepdims=True)
            exponents = jnp.where(same_window, jnp.exp(scores - highest), 0.0)
            totals = jnp.sum(exponents, axis=1, keepdims=True)
            weights = (exponents / totals).astype(jnp.bfloat16)
            return jnp.dot(weights, values_part, preferred_element_type=jnp.float32).astype(
                jnp.bfloat16
            )

        heads_out = lax.map(per_head, jnp.arange(HEADS, dtype=jnp.int32))
        results.append(jnp.transpose(heads_out, (1, 0, 2)).reshape(block_rows, channels))
    return jnp.concatenate(results, axis=0)


def sublayer(hidden, window_ids, w_qkv_layer, w_out_layer, gain_layer, temper_layer):
    local_rows = hidden.shape[0]
    channels = hidden.shape[1]
    rim_width = local_rows // 4
    marks = window_ids + 1
    factor = temper_layer * (1.0 / math.sqrt(channels // HEADS))
    projected = jnp.dot(hidden, w_qkv_layer, preferred_element_type=jnp.float32).astype(
        jnp.bfloat16
    )
    key_vals = projected[:, channels:]
    padded, marks_pad = (
        extended(key_vals, (("wide", 0),), rim_width),
        extended(marks, (("wide", 0),), rim_width),
    )
    queries = projected[:, :channels]
    attended = window_attention(queries, padded, marks, marks_pad, factor, rim_width)
    return settle(hidden, attended, w_out_layer, gain_layer)


def regroup_rows(first, dest):
    local_rows = first.shape[0]
    channels = first.shape[1]
    devices = lax.axis_size("wide")
    capacity = 2 * local_rows // devices
    target = dest // local_rows
    slot_within = dest - target * local_rows
    matches = (target[:, None] == jnp.arange(devices, dtype=jnp.int32)[None, :]).astype(jnp.int32)
    position = jnp.sum(jnp.cumsum(matches, axis=0) * matches, axis=1) - 1
    buffer_row = target * capacity + position
    outgoing = jnp.zeros((devices * capacity, channels), jnp.bfloat16).at[buffer_row].set(first)
    slot_list = (
        jnp.full((devices * capacity,), local_rows, jnp.int32).at[buffer_row].set(slot_within)
    )
    arrived, arrived_slots = (
        lax.all_to_all(outgoing, "wide", split_axis=0, concat_axis=0, tiled=True),
        lax.all_to_all(slot_list, "wide", split_axis=0, concat_axis=0, tiled=True),
    )
    return (
        jnp.zeros((local_rows, channels), jnp.bfloat16).at[arrived_slots].set(arrived, mode="drop")
    )


def body(voxels, regular_window, shifted_window, dest, w_qkv, w_out, gain, temper):
    first = sublayer(voxels, regular_window, w_qkv[0], w_out[0], gain[0], temper[0])
    moved = regroup_rows(first, dest)
    return sublayer(moved, shifted_window, w_qkv[1], w_out[1], gain[1], temper[1])


def solution(mesh):
    in_specs = (
        P(("parts", "wide"), None),
        P(("parts", "wide")),
        P(("parts", "wide")),
        P(("parts", "wide")),
        P(),
        P(),
        P(),
        P(),
    )
    out_specs = P(("parts", "wide"), None)
    return jax.shard_map(body, mesh=mesh, in_specs=in_specs, out_specs=out_specs, check_vma=False)
```

profile of v0, /device:TPU:8, one launch (start us, length us, event | category | flops | bytes accessed | tf_op | source)
XLA Modules:
  0.0 403.6 jit_solution(13931724288074019573)
XLA Ops:
  4.7 4.5 %collective-permute-start.2 = (bf16[256,512]{1,0:T(8,128)(2,1)}, bf16[256,512]{1,0:T(8,128)(2,1)}, u32[]{:S(2)}, u32[]{:S(2)}) collective-permute-start(bf16[256,512]{1,0:T(8,128)(2,1)} %get-tuple-element.522), channel_id=1, source_target_pairs={{1,0},{2,1},{3,2},{4,3},{5,4},{6,5},{7,6},{8,7},{9,8},{10,9},{11,1... | collective-permute-start | bytes 786440 | tf_op jit(solution)/shard_map/ppermute | solution.py:23
  11.2 4.5 %collective-permute-start.3 = (s32[256]{0:T(256)S(1)}, s32[256]{0:T(256)S(1)}, u32[]{:S(2)}, u32[]{:S(2)}) collective-permute-start(s32[256]{0:T(256)S(1)} %get-tuple-element.540), channel_id=1, source_target_pairs={{1,0},{2,1},{3,2},{4,3},{5,4},{6,5},{7,6},{8,7},{9,8},{10,9},{11,1... | collective-permute-start | bytes 3080 | tf_op jit(solution)/shard_map/ppermute | solution.py:23
  15.8 4.5 %reduce-window.6 = s32[16,8,128]{2,1,0:T(8,128)S(1)} reduce-window(s32[16,8,128]{2,1,0:T(8,128)S(1)} %fusion.76, s32[]{:T(128)} %constant.259.clone.1), window={size=1x1x128 pad=0_0x0_0x127_0}, to_apply=%region_0.1 | reduce-window | flops 2080768 | bytes 131076 | tf_op jit(solution)/shard_map/reduce-window
  20.8 4.9 %scatter_custom_fusion = s32[2048]{0:T(1024)} fusion(s32[1024]{0:T(1024)S(1)} %get-tuple-element.542, s32[1024]{0:T(1024)S(1)} %get-tuple-element.541, s32[]{:T(128)} %constant.257.clone.1), kind=kCustom, calls=%fused_computation.123 | custom fusion | bytes 8196 | tf_op jit(solution)/shard_map/scatter | solution.py:109
  25.6 5.3 %all-to-all-start = ((s32[16,128,1]{1,2,0:T(1,128)}), s32[16,128,1]{1,2,0:T(1,128)S(1)}, u32[]{:S(2)}, u32[]{:S(2)}) async-start(s32[16,128,1]{1,2,0:T(1,128)} %bitcast.4), calls=%async_computation | async-start | bytes 16384 | tf_op jit(solution)/shard_map/all_to_all | solution.py:113
  35.5 78.1 %while.52 = (s32[]{:T(128)}, bf16[8,512,32]{1,2,0:T(8,128)(2,1)S(1)}, s32[8]{0:T(128)S(1)}, bf16[512,256]{1,0:T(8,128)(2,1)}, bf16[1024,512]{1,0:T(8,128)(2,1)},...) while((s32[]{:T(128)}, ...), condition=%wide.region_7.8_spmd.clone, body=%wide.region_4.7_spmd.clone.sunk | while | flops 76037128 | bytes 7010112 | solution.py:73
  42.7 2.5 fusion.116
  52.5 2.5 fusion.116
  62.2 2.5 fusion.116
  72.0 2.5 fusion.116
  81.8 2.5 fusion.116
  91.5 2.5 fusion.116
  101.3 2.5 fusion.116
  111.0 2.5 fusion.116
  113.6 74.5 %while.53 = (s32[]{:T(128)}, bf16[8,512,32]{1,2,0:T(8,128)(2,1)S(1)}, s32[8]{0:T(128)S(1)}, bf16[512,256]{1,0:T(8,128)(2,1)}, bf16[1024,512]{1,0:T(8,128)(2,1)},...) while((s32[]{:T(128)}, ...), condition=%wide.region_11.12_spmd.clone, body=%wide.region_8.11_spmd.clone.sunk | while | flops 76037128 | bytes 7010112 | solution.py:73
  189.1 6.0 %scatter_custom_fusion.1 = bf16[2048,256]{1,0:T(8,128)(2,1)} fusion(s32[1024]{0:T(1024)S(1)} %get-tuple-element.542, bf16[1024,256]{1,0:T(8,128)(2,1)S(1)} %copy.23, bf16[]{:T(256)} %constant.256.clone.1), kind=kCustom, calls=%fused_computation.89 | custom fusion | bytes 1048578 | tf_op jit(solution)/shard_map/scatter | solution.py:107
  195.1 6.0 %all-to-all-start.1 = ((bf16[16,128,256]{2,1,0:T(8,128)(2,1)}), bf16[16,128,256]{2,1,0:T(8,128)(2,1)S(1)}, u32[]{:S(2)}, u32[]{:S(2)}) async-start(bf16[16,128,256]{2,1,0:T(8,128)(2,1)} %bitcast.15), calls=%async_computation.1 | async-start | bytes 2097152 | tf_op jit(solution)/shard_map/all_to_all | solution.py:112
  203.2 4.6 %collective-permute-start.7 = (s32[256]{0:T(256)S(1)}, s32[256]{0:T(256)S(1)}, u32[]{:S(2)}, u32[]{:S(2)}) collective-permute-start(s32[256]{0:T(256)S(1)} %get-tuple-element.534), channel_id=1, source_target_pairs={{1,0},{2,1},{3,2},{4,3},{5,4},{6,5},{7,6},{8,7},{9,8},{10,9},{11,1... | collective-permute-start | bytes 3080 | tf_op jit(solution)/shard_map/ppermute | solution.py:23
  207.8 17.5 %all-to-all-done.1 = bf16[16,128,256]{2,1,0:T(8,128)(2,1)S(1)} async-done(((bf16[16,128,256]{2,1,0:T(8,128)(2,1)}), bf16[16,128,256]{2,1,0:T(8,128)(2,1)S(1)}, u32[]{:S(2)}, u32[]{:S(2)}) %all-to-all-start.1) | async-done | bytes 1048608 | tf_op jit(solution)/shard_map/all_to_all | solution.py:112
  225.3 9.4 %scatter_custom_fusion.2 = bf16[1024,256]{1,0:T(8,128)(2,1)S(1)} fusion(s32[2048]{0:T(1024)S(1)} %bitcast.115, bf16[2048,256]{1,0:T(8,128)(2,1)S(1)} %bitcast.112, bf16[]{:T(256)} %constant.256.clone.1), kind=kCustom, calls=%fused_computation.95 | custom fusion | bytes 524290 | tf_op jit(solution)/shard_map/scatter | solution.py:116
  236.1 2.7 collective-permute-start.4
  238.8 3.8 collective-permute-start.6
  249.3 78.1 %while.54 = (s32[]{:T(128)}, bf16[8,512,32]{1,2,0:T(8,128)(2,1)S(1)}, s32[8]{0:T(128)S(1)}, bf16[512,256]{1,0:T(8,128)(2,1)}, bf16[1024,512]{1,0:T(8,128)(2,1)},...) while((s32[]{:T(128)}, ...), condition=%wide.region_19.20_spmd.clone, body=%wide.region_16.19_spmd.clone.sunk | while | flops 76037128 | bytes 7010112 | solution.py:73
  327.4 74.5 %while.55 = (s32[]{:T(128)}, bf16[8,512,32]{1,2,0:T(8,128)(2,1)S(1)}, s32[8]{0:T(128)S(1)}, bf16[512,256]{1,0:T(8,128)(2,1)}, bf16[1024,512]{1,0:T(8,128)(2,1)},...) while((s32[]{:T(128)}, ...), condition=%wide.region_23.24_spmd.clone, body=%wide.region_20.23_spmd.clone.sunk | while | flops 76037128 | bytes 7010112 | solution.py:73
  (239 shorter events, 232.5 us)
Async XLA Ops:
  0.0 9.2 %copy-start.7 = (s32[1024]{0:T(1024)S(1)}, s32[1024]{0:T(1024)}, u32[]{:S(2)}) copy-start(s32[1024]{0:T(1024)} %param.17) | copy-start | bytes 12292
  0.0 15.7 %copy-start.6 = (s32[1024]{0:T(1024)S(1)}, s32[1024]{0:T(1024)}, u32[]{:S(2)}) copy-start(s32[1024]{0:T(1024)} %param.19) | copy-start | bytes 12292
  0.0 31.8 %copy-start.9 = (f32[2,256]{1,0:T(2,128)S(1)}, f32[2,256]{1,0:T(2,128)}, u32[]{:S(2)}) copy-start(f32[2,256]{1,0:T(2,128)} %param.22) | copy-start | bytes 6148
  0.0 31.8 %copy-start.10 = (f32[2,8]{1,0:T(2,128)S(1)}, f32[2,8]{1,0:T(2,128)}, u32[]{:S(2)}) copy-start(f32[2,8]{1,0:T(2,128)} %param.23) | copy-start | bytes 196
  2.6 29.3 %copy-start = (bf16[1024,256]{1,0:T(8,128)(2,1)S(1)}, bf16[1024,256]{1,0:T(8,128)(2,1)}, u32[]{:S(2)}) copy-start(bf16[1024,256]{1,0:T(8,128)(2,1)} %param.16) | copy-start | bytes 1572868
  2.6 30.3 %collective-permute-start = (bf16[256,512]{1,0:T(8,128)(2,1)}, bf16[256,512]{1,0:T(8,128)(2,1)S(1)}, u32[]{:S(2)}, u32[]{:S(2)}) collective-permute-start(bf16[256,512]{1,0:T(8,128)(2,1)} %get-tuple-element.521), channel_id=1, source_target_pairs={{0,1},{1,2},{2,3},{3,4},{4,5},{5,6},{6,7},{7,8},{8,9},{9,10},{10,1... | collective-permute-start | bytes 786440 | tf_op jit(solution)/shard_map/ppermute | solution.py:20
  4.7 28.3 %collective-permute-start.2 = (bf16[256,512]{1,0:T(8,128)(2,1)}, bf16[256,512]{1,0:T(8,128)(2,1)}, u32[]{:S(2)}, u32[]{:S(2)}) collective-permute-start(bf16[256,512]{1,0:T(8,128)(2,1)} %get-tuple-element.522), channel_id=1, source_target_pairs={{1,0},{2,1},{3,2},{4,3},{5,4},{6,5},{7,6},{8,7},{9,8},{10,9},{11,1... | collective-permute-start | bytes 786440 | tf_op jit(solution)/shard_map/ppermute | solution.py:23
  9.2 23.7 %collective-permute-start.1 = (s32[256]{0:T(256)S(1)}, s32[256]{0:T(256)S(1)}, u32[]{:S(2)}, u32[]{:S(2)}) collective-permute-start(s32[256]{0:T(256)S(1)} %get-tuple-element.539), channel_id=1, source_target_pairs={{0,1},{1,2},{2,3},{3,4},{4,5},{5,6},{6,7},{7,8},{8,9},{9,10},{10,1... | collective-permute-start | bytes 3080 | tf_op jit(solution)/shard_map/ppermute | solution.py:20
  11.2 21.8 %collective-permute-start.3 = (s32[256]{0:T(256)S(1)}, s32[256]{0:T(256)S(1)}, u32[]{:S(2)}, u32[]{:S(2)}) collective-permute-start(s32[256]{0:T(256)S(1)} %get-tuple-element.540), channel_id=1, source_target_pairs={{1,0},{2,1},{3,2},{4,3},{5,4},{6,5},{7,6},{8,7},{9,8},{10,9},{11,1... | collective-permute-start | bytes 3080 | tf_op jit(solution)/shard_map/ppermute | solution.py:23
  25.6 169.5 %all-to-all-start = ((s32[16,128,1]{1,2,0:T(1,128)}), s32[16,128,1]{1,2,0:T(1,128)S(1)}, u32[]{:S(2)}, u32[]{:S(2)}) async-start(s32[16,128,1]{1,2,0:T(1,128)} %bitcast.4), calls=%async_computation | async-start | bytes 16384 | tf_op jit(solution)/shard_map/all_to_all | solution.py:113
  113.6 74.5 %copy-start.1 = (bf16[1024,256]{0,1:T(8,128)(2,1)S(1)}, bf16[1024,256]{0,1:T(8,128)(2,1)}, u32[]{:S(2)}) copy-start(bf16[1024,256]{0,1:T(8,128)(2,1)} %copy.22) | copy-start | bytes 1572868
  113.6 74.5 %copy-start.4 = (bf16[2,256,256]{2,1,0:T(8,128)(2,1)S(1)}, bf16[2,256,256]{2,1,0:T(8,128)(2,1)}, u32[]{:S(2)}) copy-start(bf16[2,256,256]{2,1,0:T(8,128)(2,1)} %param.21) | copy-start | bytes 786436
  188.8 12.3 %copy-start.8 = (s32[1024]{0:T(1024)S(1)}, s32[1024]{0:T(1024)}, u32[]{:S(2)}) copy-start(s32[1024]{0:T(1024)} %param.18) | copy-start | bytes 12292
  189.0 45.7 %copy-start.3 = (bf16[2,256,768]{2,1,0:T(8,128)(2,1)S(1)}, bf16[2,256,768]{2,1,0:T(8,128)(2,1)}, u32[]{:S(2)}) copy-start(bf16[2,256,768]{2,1,0:T(8,128)(2,1)} %param.20) | copy-start | bytes 2359300
  195.1 30.2 %all-to-all-start.1 = ((bf16[16,128,256]{2,1,0:T(8,128)(2,1)}), bf16[16,128,256]{2,1,0:T(8,128)(2,1)S(1)}, u32[]{:S(2)}, u32[]{:S(2)}) async-start(bf16[16,128,256]{2,1,0:T(8,128)(2,1)} %bitcast.15), calls=%async_computation.1 | async-start | bytes 2097152 | tf_op jit(solution)/shard_map/all_to_all | solution.py:112
  201.2 41.4 %collective-permute-start.5 = (s32[256]{0:T(256)S(1)}, s32[256]{0:T(256)S(1)}, u32[]{:S(2)}, u32[]{:S(2)}) collective-permute-start(s32[256]{0:T(256)S(1)} %get-tuple-element.533), channel_id=1, source_target_pairs={{0,1},{1,2},{2,3},{3,4},{4,5},{5,6},{6,7},{7,8},{8,9},{9,10},{10,1... | collective-permute-start | bytes 3080 | tf_op jit(solution)/shard_map/ppermute | solution.py:20
  203.2 39.4 %collective-permute-start.7 = (s32[256]{0:T(256)S(1)}, s32[256]{0:T(256)S(1)}, u32[]{:S(2)}, u32[]{:S(2)}) collective-permute-start(s32[256]{0:T(256)S(1)} %get-tuple-element.534), channel_id=1, source_target_pairs={{1,0},{2,1},{3,2},{4,3},{5,4},{6,5},{7,6},{8,7},{9,8},{10,9},{11,1... | collective-permute-start | bytes 3080 | tf_op jit(solution)/shard_map/ppermute | solution.py:23
  236.1 8.8 %collective-permute-start.4 = (bf16[256,512]{1,0:T(8,128)(2,1)}, bf16[256,512]{1,0:T(8,128)(2,1)S(1)}, u32[]{:S(2)}, u32[]{:S(2)}) collective-permute-start(bf16[256,512]{1,0:T(8,128)(2,1)} %get-tuple-element.517), channel_id=1, source_target_pairs={{0,1},{1,2},{2,3},{3,4},{4,5},{5,6},{6,7},{7,8},{8,9},{9,10},{10,1... | collective-permute-start | bytes 786440 | tf_op jit(solution)/shard_map/ppermute | solution.py:20
  238.8 8.0 %collective-permute-start.6 = (bf16[256,512]{1,0:T(8,128)(2,1)}, bf16[256,512]{1,0:T(8,128)(2,1)}, u32[]{:S(2)}, u32[]{:S(2)}) collective-permute-start(bf16[256,512]{1,0:T(8,128)(2,1)} %get-tuple-element.518), channel_id=1, source_target_pairs={{1,0},{2,1},{3,2},{4,3},{5,4},{6,5},{7,6},{8,7},{9,8},{10,9},{11,1... | collective-permute-start | bytes 786440 | tf_op jit(solution)/shard_map/ppermute | solution.py:23
  327.4 74.5 %copy-start.2 = (bf16[1024,256]{0,1:T(8,128)(2,1)S(1)}, bf16[1024,256]{0,1:T(8,128)(2,1)}, u32[]{:S(2)}) copy-start(bf16[1024,256]{0,1:T(8,128)(2,1)} %copy.24) | copy-start | bytes 1572868
  327.4 74.5 %copy-start.5 = (bf16[2,256,256]{2,1,0:T(8,128)(2,1)S(1)}, bf16[2,256,256]{2,1,0:T(8,128)(2,1)}, u32[]{:S(2)}) copy-start(bf16[2,256,256]{2,1,0:T(8,128)(2,1)} %param.21) | copy-start | bytes 786436
where the time goes:
time: 410 us; the launch traced here: 404 us
  matrix products  153 us (37%)
  loops' own time  76.8 us (19%)
  local copies, waits for them, and re-layouts  65 us (16%)
  other arithmetic  50.9 us (12%)
  starting transfers between devices  37.5 us (9%)
  waiting for transfers between devices  19.7 us (5%)
    dot_general x32, matrix products, per_head(): jnp.dot(weights, values_part, preferred_element_type=jnp.float32)  79.2 us
    another operation x4, loops' own time, window_attention(): heads_out = lax.map(per_head, jnp.arange(HEADS, dtype=jnp.int32))  76.8 us
    dot_general x32, matrix products, per_head(): lax.dot_general(query_part, keys_part, (((1,), (1,)), ((), ())), preferre...  71 us
    reduce_sum x32, other arithmetic, per_head(): totals = jnp.sum(exponents, axis=1, keepdims=True)  40.6 us
    dynamic_slice x32, local copies, waits for them, and re-layouts, window_attention(): heads_out = lax.map(per_head, jnp.arange(HEADS, dtype=jnp.int32))  18.8 us
    dynamic_slice x32, local copies, waits for them, and re-layouts, per_head(): scores = scores * factor[head_index]  18.8 us
    all_to_all x1, waiting for transfers between devices, regroup_rows(): lax.all_to_all(outgoing, 'wide', split_axis=0, concat_axis=0, tiled=True)  17.5 us
    ppermute x4, starting transfers between devices, extended(): lax.ppermute(lax.slice_in_dim(block, 0, width, axis=dim), axis, backward)  17.5 us
  transfers between devices with their start and end apart: 10, of which 3 were waited for; matrix products, arithmetic and copies ran while one was open for 37% of the time, Pallas kernels for 0%

commit v1 on v0

v1 whole, which is shorter than its diff:
```python
import functools
import math

import jax
import jax.numpy as jnp
from jax import lax
from jax.experimental import pallas as pl
from jax.experimental.pallas import tpu as pltpu
from jax.sharding import PartitionSpec as P

HEADS = 8
TILE = 128

epsilon = 1e-05
masked_score = -1e30
no_mark = 1 << 30

vmem = pl.BlockSpec(memory_space=pltpu.VMEM)
smem = pl.BlockSpec(memory_space=pltpu.SMEM)


def dot(a, b):
    return jnp.dot(a, b, preferred_element_type=jnp.float32)


def dot_t(a, b):
    return lax.dot_general(a, b, (((1,), (1,)), ((), ())), preferred_element_type=jnp.float32)


def ranks(match):
    rows, columns = match.shape
    before = (
        lax.broadcasted_iota(jnp.int32, (TILE, TILE), 0)
        < lax.broadcasted_iota(jnp.int32, (TILE, TILE), 1)
    ).astype(jnp.bfloat16)
    carry = jnp.zeros((rows, 1), jnp.float32)
    pieces = []
    for start in range(0, columns, TILE):
        piece = match[:, start : start + TILE]
        pieces.append(dot(piece.astype(jnp.bfloat16), before) + carry)
        carry = carry + jnp.sum(piece, axis=1, keepdims=True)
    return jnp.concatenate(pieces, axis=1)


def one_hot(hits):
    return jnp.where(hits, 1.0, 0.0).astype(jnp.bfloat16)


def attend_tile(number, span_ref, scale_ref, marks_ref, query_ref, keyval_ref, attended_ref, rim):
    channels = query_ref.shape[1]
    head_dim = channels // HEADS
    per_group = TILE // head_dim
    groups = channels // TILE
    row = pl.multiple_of(number * TILE, TILE)
    low = span_ref[0, number]
    count = span_ref[1, number]
    most = 1 + 2 * (rim // TILE)
    lane_head = lax.broadcasted_iota(jnp.int32, (TILE, TILE), 1) // head_dim
    own = marks_ref[pl.ds(number + rim // TILE, 1), :]
    own = jnp.transpose(jnp.broadcast_to(own, (TILE, TILE)))

    def variant(tiles):
        first_key = pl.multiple_of(low * TILE, TILE)
        same = [own == marks_ref[pl.ds(low + i, 1), :] for i in range(tiles)]
        same = jnp.concatenate(same, axis=1)
        for group in range(groups):
            lanes = slice(group * TILE, (group + 1) * TILE)
            query = query_ref[pl.ds(row, TILE), lanes]
            stacked = jnp.concatenate(
                [jnp.where(lane_head == j, query, 0.0).astype(jnp.bfloat16) for j in range(per_group)],
                axis=0,
            )
            keys = keyval_ref[pl.ds(first_key, tiles * TILE), lanes]
            values = keyval_ref[
                pl.ds(first_key, tiles * TILE),
                channels + group * TILE : channels + (group + 1) * TILE,
            ]
            scores = dot_t(stacked, keys)
            weights = []
            for j in range(per_group):
                part = scores[j * TILE : (j + 1) * TILE] * scale_ref[group * per_group + j]
                part = jnp.where(same, part, masked_score)
                part = jnp.exp2(part - jnp.max(part, axis=1, keepdims=True))
                part = part * (1.0 / jnp.sum(part, axis=1, keepdims=True))
                weights.append(part.astype(jnp.bfloat16))
            mixed = dot(jnp.concatenate(weights, axis=0), values)
            total = mixed[:TILE]
            for j in range(1, per_group):
                total = jnp.where(lane_head == j, mixed[j * TILE : (j + 1) * TILE], total)
            attended_ref[pl.ds(row, TILE), lanes] = total.astype(jnp.bfloat16)

    for tiles in range(2, most + 1):
        pl.when(jnp.maximum(count, 2) == tiles)(functools.partial(variant, tiles))


def sublayer_kernel(
    packing, span_ref, scale_ref, marks_ref, dest_ref, low_ref, hidden_ref, high_ref, w_qkv_ref,
    w_out_ref, gain_ref, out_ref, query_ref, keyval_ref, attended_ref, first_ref,
):
    rows, channels = hidden_ref.shape
    rim = low_ref.shape[0]
    chunk = min(256, rows)
    for start in range(0, rows, chunk):
        projected = dot(hidden_ref[start : start + chunk], w_qkv_ref[...]).astype(jnp.bfloat16)
        query_ref[start : start + chunk] = projected[:, :channels]
        keyval_ref[rim + start : rim + start + chunk] = projected[:, channels:]
    keyval_ref[:rim] = dot(low_ref[...], w_qkv_ref[:, channels:]).astype(jnp.bfloat16)
    keyval_ref[rim + rows :] = dot(high_ref[...], w_qkv_ref[:, channels:]).astype(jnp.bfloat16)

    def one_tile(number, nothing):
        attend_tile(
            number, span_ref, scale_ref, marks_ref, query_ref, keyval_ref, attended_ref, rim
        )
        return nothing

    lax.fori_loop(0, rows // TILE, one_tile, 0)
    final_ref = first_ref if packing else out_ref
    for start in range(0, rows, chunk):
        here = slice(start, start + chunk)
        summed = hidden_ref[here].astype(jnp.float32) + dot(attended_ref[here], w_out_ref[...])
        center = jnp.mean(summed, axis=1, keepdims=True)
        summed = summed - center
        spread = jnp.mean(jnp.square(summed), axis=1, keepdims=True)
        final_ref[here] = (summed * lax.rsqrt(spread + epsilon) * gain_ref[...]).astype(jnp.bfloat16)
    if not packing:
        return
    devices = packing
    capacity = 2 * rows // devices
    target = dest_ref[...] // rows
    match = jnp.where(
        lax.broadcasted_iota(jnp.int32, (devices, rows), 0) == target, 1.0, 0.0
    )
    place = jnp.sum(ranks(match) * match, axis=0, keepdims=True).astype(jnp.int32)
    place = place + target * capacity
    for start in range(0, devices * capacity, TILE):
        index = lax.broadcasted_iota(jnp.int32, (TILE, rows), 0) + start
        out_ref[start : start + TILE] = dot(one_hot(index == place), first_ref[...]).astype(
            jnp.bfloat16
        )


def run_sublayer(hidden, low, high, marks, spans, dest, w_qkv, w_out, gain, temper, packing):
    rows, channels = hidden.shape
    rim = low.shape[0]
    scale = temper * (1.0 / math.sqrt(channels // HEADS)) * math.log2(math.e)
    out_rows = 2 * rows if packing else rows
    return pl.pallas_call(
        functools.partial(sublayer_kernel, packing),
        out_shape=jax.ShapeDtypeStruct((out_rows, channels), jnp.bfloat16),
        in_specs=[smem, smem] + [vmem] * 8,
        out_specs=vmem,
        scratch_shapes=[
            pltpu.VMEM((rows, channels), jnp.bfloat16),
            pltpu.VMEM((rows + 2 * rim, 2 * channels), jnp.bfloat16),
            pltpu.VMEM((rows, channels), jnp.bfloat16),
            pltpu.VMEM((rows, channels), jnp.bfloat16),
        ],
        compiler_params=pltpu.CompilerParams(vmem_limit_bytes=40 * 1024 * 1024),
        cost_estimate=pl.CostEstimate(
            flops=8 * 10**9, bytes_accessed=4 * 10**6, transcendentals=8 * 10**6
        ),
        name="sublayer",
    )(
        spans, scale, marks.reshape(-1, TILE), dest.reshape(1, rows), low, hidden, high, w_qkv,
        w_out, gain.reshape(1, channels),
    )


def slots_kernel(capacity, base_ref, dest_ref, slots_ref):
    devices, rows = dest_ref.shape
    slot = dest_ref[...] - base_ref[0]
    inside = (slot >= 0) & (slot < rows)
    match = jnp.where(inside, 1.0, 0.0)
    rank = jnp.where(inside, ranks(match).astype(jnp.int32), -1)
    slot = jnp.where(inside, slot, 0)
    which = lax.broadcasted_iota(jnp.int32, (16, rows), 0)
    place = lax.broadcasted_iota(jnp.int32, (capacity, rows), 0)
    for source in range(devices):
        own = slot[source : source + 1]
        digits = jnp.where(
            which == 0, own // 32, jnp.where(which == 1, own % 32, jnp.where(which == 2, 1, 0))
        )
        hits = one_hot(place == rank[source : source + 1])
        found = dot_t(digits.astype(jnp.float32).astype(jnp.bfloat16), hits)
        value = found[0:1] * 32.0 + found[1:2] + (found[2:3] - 1.0) * 2048.0
        slots_ref[source : source + 1] = value.astype(jnp.int32)


def run_slots(base, dest_all, capacity):
    devices = dest_all.shape[0]
    return pl.pallas_call(
        functools.partial(slots_kernel, capacity),
        out_shape=jax.ShapeDtypeStruct((devices, capacity), jnp.int32),
        in_specs=[smem, vmem],
        out_specs=vmem,
        compiler_params=pltpu.CompilerParams(vmem_limit_bytes=40 * 1024 * 1024),
        cost_estimate=pl.CostEstimate(flops=2 * 10**9, bytes_accessed=10**6, transcendentals=0),
        name="slots",
    )(base, dest_all)


def place_kernel(slots_ref, arrived_ref, moved_ref):
    rows = moved_ref.shape[0]
    parts = slots_ref.shape[0]
    for start in range(0, rows, TILE):
        index = lax.broadcasted_iota(jnp.int32, (TILE, TILE), 0) + start
        hits = jnp.concatenate([one_hot(index == slots_ref[i : i + 1]) for i in range(parts)], axis=1)
        moved_ref[start : start + TILE] = dot(hits, arrived_ref[...]).astype(jnp.bfloat16)


def run_place(slots, arrived, rows):
    return pl.pallas_call(
        place_kernel,
        out_shape=jax.ShapeDtypeStruct((rows, arrived.shape[1]), jnp.bfloat16),
        in_specs=[vmem, vmem],
        out_specs=vmem,
        compiler_params=pltpu.CompilerParams(vmem_limit_bytes=40 * 1024 * 1024),
        cost_estimate=pl.CostEstimate(
            flops=10**9, bytes_accessed=2 * 10**6, transcendentals=0
        ),
        name="place",
    )(slots.reshape(-1, TILE), arrived)


def neighbours(block, width, axis):
    count = lax.axis_size("wide")
    forward = [(i, i + 1) for i in range(count - 1)]
    backward = [(target, source) for source, target in forward]
    size = block.shape[axis]
    low = lax.ppermute(lax.slice_in_dim(block, size - width, size, axis=axis), "wide", forward)
    high = lax.ppermute(lax.slice_in_dim(block, 0, width, axis=axis), "wide", backward)
    return low, high


def extents(marks, low, high):
    high = jnp.where(high == 0, no_mark, high)
    padded = jnp.concatenate([low, marks, high])
    begin = jnp.sum((padded[None, :] < marks[::TILE, None]).astype(jnp.int32), axis=1) // TILE
    end = jnp.sum((padded[None, :] <= marks[TILE - 1 :: TILE, None]).astype(jnp.int32), axis=1)
    end = (end + TILE - 1) // TILE
    return padded, jnp.stack([begin, end - begin])


def body(voxels, regular_window, shifted_window, dest, w_qkv, w_out, gain, temper):
    rows, channels = voxels.shape
    rim = rows // 4
    devices = lax.axis_size("wide")
    capacity = 2 * rows // devices
    base = lax.axis_index("wide").astype(jnp.int32).reshape(1) * rows
    low, high = neighbours(voxels, rim, 0)
    marks = jnp.stack([regular_window, shifted_window]) + 1
    marks_low, marks_high = neighbours(marks, rim, 1)
    dest_all = lax.all_gather(dest, "wide")
    marks_first, spans_first = extents(marks[0], marks_low[0], marks_high[0])
    marks_second, spans_second = extents(marks[1], marks_low[1], marks_high[1])
    outgoing = run_sublayer(
        voxels, low, high, marks_first, spans_first, dest, w_qkv[0], w_out[0], gain[0], temper[0],
        devices,
    )
    arrived = lax.all_to_all(outgoing, "wide", split_axis=0, concat_axis=0, tiled=True)
    slots = run_slots(base, dest_all, capacity)
    moved = run_place(slots, arrived, rows)
    low, high = neighbours(moved, rim, 0)
    return run_sublayer(
        moved, low, high, marks_second, spans_second, dest, w_qkv[1], w_out[1], gain[1], temper[1],
        0,
    )


def solution(mesh):
    in_specs = (
        P(("parts", "wide"), None),
        P(("parts", "wide")),
        P(("parts", "wide")),
        P(("parts", "wide")),
        P(),
        P(),
        P(),
        P(),
    )
    out_specs = P(("parts", "wide"), None)
    return jax.shard_map(body, mesh=mesh, in_specs=in_specs, out_specs=out_specs, check_vma=False)
```

time: 410 us -> 102 us (0.25)
  the two profiles are of different devices: /device:TPU:8 before, /device:TPU:13 now
where the time goes in v1:
time: 102 us; the launch traced here: 101 us
  blocking collectives  34.3 us (34%)
  Pallas kernels  32 us (31%)
  starting transfers between devices  22.4 us (22%)
  waiting for transfers between devices  7.25 us (7%)
  local copies, waits for them, and re-layouts  4.05 us (4%)
  other arithmetic  1.24 us (1%)
    all_gather x1, blocking collectives, body(): dest_all = lax.all_gather(dest, 'wide')  34.3 us
    pallas_call x2, Pallas kernels, run_sublayer(): pl.pallas_call(functools.partial(sublayer_kernel, packing), out_shape=jax...  29.4 us
    ppermute x3, starting transfers between devices, neighbours(): lax.ppermute(lax.slice_in_dim(block, size - width, size, axis=axis), 'wid...  9.85 us
    ppermute x3, waiting for transfers between devices, neighbours(): lax.ppermute(lax.slice_in_dim(block, 0, width, axis=axis), 'wide', backward)  7.24 us
    ppermute x3, starting transfers between devices, neighbours(): lax.ppermute(lax.slice_in_dim(block, 0, width, axis=axis), 'wide', backward)  7.09 us
    all_to_all x1, starting transfers between devices, body(): lax.all_to_all(outgoing, 'wide', split_axis=0, concat_axis=0, tiled=True)  5.42 us
  transfers between devices with their start and end apart: 7, of which 2 were waited for; matrix products, arithmetic and copies ran while one was open for 3% of the time, Pallas kernels for 1%

profile of v1, /device:TPU:13, one launch (start us, length us, event | category | flops | bytes accessed | tf_op | source)
XLA Modules:
  0.0 101.5 jit_solution(8879607167692749564)
XLA Ops:
  0.0 0.7 add_add_fusion
  0.7 2.6 %collective-permute-start.1 = (s32[2,256]{1,0:T(2,128)S(1)}, s32[2,256]{1,0:T(2,128)S(1)}, u32[]{:S(2)}, u32[]{:S(2)}) collective-permute-start(s32[2,256]{1,0:T(2,128)S(1)} %get-tuple-element.20), channel_id=1, source_target_pairs={{1,0},{2,1},{3,2},{4,3},{5,4},{6,5},{7,6},{8,7},{9,8},{10,9},{11,1... | collective-permute-start | bytes 6152 | tf_op jit(solution)/shard_map/ppermute | solution.py:231
  3.3 3.9 %collective-permute-start = (s32[2,256]{1,0:T(2,128)S(1)}, s32[2,256]{1,0:T(2,128)S(1)}, u32[]{:S(2)}, u32[]{:S(2)}) collective-permute-start(s32[2,256]{1,0:T(2,128)S(1)} %get-tuple-element.19), channel_id=1, source_target_pairs={{0,1},{1,2},{2,3},{3,4},{4,5},{5,6},{6,7},{7,8},{8,9},{9,10},{10,1... | collective-permute-start | bytes 6152 | tf_op jit(solution)/shard_map/ppermute | solution.py:230
  7.2 1.0 fusion.5
  8.2 1.9 %collective-permute-start.2 = (bf16[256,256]{1,0:T(8,128)(2,1)S(1)}, bf16[256,256]{1,0:T(8,128)(2,1)S(1)}, u32[]{:S(2)}, u32[]{:S(2)}) collective-permute-start(bf16[256,256]{1,0:T(8,128)(2,1)S(1)} %get-tuple-element.14), channel_id=1, source_target_pairs={{0,1},{1,2},{2,3},{3,4},{4,5},{5,6},{6,7},{7,8},{8,9},{9,10},{10,1... | collective-permute-start | bytes 393224 | tf_op jit(solution)/shard_map/ppermute | solution.py:230
  10.1 2.4 %collective-permute-start.3 = (bf16[256,256]{1,0:T(8,128)(2,1)S(1)}, bf16[256,256]{1,0:T(8,128)(2,1)S(1)}, u32[]{:S(2)}, u32[]{:S(2)}) collective-permute-start(bf16[256,256]{1,0:T(8,128)(2,1)S(1)} %get-tuple-element.13), channel_id=1, source_target_pairs={{1,0},{2,1},{3,2},{4,3},{5,4},{6,5},{7,6},{8,7},{9,8},{10,9},{11,1... | collective-permute-start | bytes 393224 | tf_op jit(solution)/shard_map/ppermute | solution.py:231
  12.6 1.2 %slice_bitcast_fusion = (bf16[256,768]{1,0:T(8,128)(2,1)S(1)}, bf16[256,768]{1,0:T(8,128)(2,1)S(1)}) fusion(bf16[2,256,768]{2,1,0:T(8,128)(2,1)} %param.12), kind=kLoop, calls=%fused_computation | loop fusion | bytes 1572864 | tf_op jit(solution)/shard_map/squeeze | solution.py:265
  13.9 0.7 copy-done.4
  14.6 0.1 slice.83
  14.7 0.1 slice.84
  14.8 0.2 convert_reduce_fusion.1
  15.1 2.2 %collective-permute-done.3.high_ref = bf16[256,256]{1,0:T(8,128)(2,1)S(1)} collective-permute-done((bf16[256,256]{1,0:T(8,128)(2,1)S(1)}, bf16[256,256]{1,0:T(8,128)(2,1)S(1)}, u32[]{:S(2)}, u32[]{:S(2)}) %collective-permute-start.3) | collective-permute-done | bytes 131104 | tf_op jit(solution)/shard_map/ppermute | solution.py:231
  17.3 0.7 copy-done.1
  18.0 14.9 %sublayer.2 = bf16[2048,256]{1,0:T(8,128)(2,1)} custom-call(s32[2,8]{1,0:T(2,128)S(1)} %pad_add_fusion.3.span_ref, f32[8]{0:T(128)S(1)} %get-tuple-element.31.scale_ref, s32[12,128]{1,0:T(8,128)S(1)} %get-tuple-element.21.marks_ref, s32[1,1024]{1,0:T(1,128)S(1)} %bitcast.69, bf16[256,256]{1,0:T(8,128)(2,1)S(1)} %collective-permute-done.2.low_ref, ...), custom_call_target="tpu_custom_call" | custom-call | flops 8000000000 | bytes 4000000 | tf_op jit(solution)/shard_map/sublayer/pallas_call | solution.py:147
  32.9 5.4 %all-to-all-start = ((bf16[16,128,256]{2,1,0:T(8,128)(2,1)}), bf16[16,128,256]{2,1,0:T(8,128)(2,1)S(1)}, u32[]{:S(2)}, u32[]{:S(2)}) async-start(bf16[16,128,256]{2,1,0:T(8,128)(2,1)} %bitcast.20), calls=%async_computation | async-start | bytes 2097152 | tf_op jit(solution)/shard_map/all_to_all | solution.py:260
  38.4 0.1 slice.78
  38.5 34.3 %all-gather = s32[16384]{0:T(1024)S(1)} all-gather(s32[1024]{0:T(1024)S(1)} %copy-done.1), channel_id=2, replica_groups=mesh['parts'=2,'wide'=16] {'wide'}, dimensions={0}, use_global_device_ids=true | all-gather | bytes 69632 | tf_op jit(solution)/shard_map/all_gather | solution.py:253
  72.9 1.3 %slots.1.slots_ref = s32[16,128]{1,0:T(8,128)S(1)} custom-call(s32[1]{0:T(128)} %bitcast.10.base_ref, s32[16,1024]{1,0:T(8,128)S(1)} %reshape.248.dest_ref), custom_call_target="tpu_custom_call" | custom-call | flops 2000000000 | bytes 1000000 | tf_op jit(solution)/shard_map/slots/pallas_call | solution.py:191
  74.3 0.2 convert_reduce_fusion.3
  74.5 1.3 %place.1.hidden_ref = bf16[1024,256]{1,0:T(8,128)(2,1)S(1)} custom-call(s32[16,128]{1,0:T(8,128)S(1)} %slots.1.slots_ref, bf16[2048,256]{1,0:T(8,128)(2,1)S(1)} %bitcast.68), custom_call_target="tpu_custom_call" | custom-call | flops 1000000000 | bytes 2000000 | tf_op jit(solution)/shard_map/place/pallas_call | solution.py:212
  75.8 4.1 %collective-permute-start.4 = (bf16[256,256]{1,0:T(8,128)(2,1)S(1)}, bf16[256,256]{1,0:T(8,128)(2,1)S(1)}, u32[]{:S(2)}, u32[]{:S(2)}) collective-permute-start(bf16[256,256]{1,0:T(8,128)(2,1)S(1)} %get-tuple-element.12), channel_id=1, source_target_pairs={{0,1},{1,2},{2,3},{3,4},{4,5},{5,6},{6,7},{7,8},{8,9},{9,10},{10,1... | collective-permute-start | bytes 393224 | tf_op jit(solution)/shard_map/ppermute | solution.py:230
  79.8 2.1 %collective-permute-start.5 = (bf16[256,256]{1,0:T(8,128)(2,1)S(1)}, bf16[256,256]{1,0:T(8,128)(2,1)S(1)}, u32[]{:S(2)}, u32[]{:S(2)}) collective-permute-start(bf16[256,256]{1,0:T(8,128)(2,1)S(1)} %get-tuple-element.11), channel_id=1, source_target_pairs={{1,0},{2,1},{3,2},{4,3},{5,4},{6,5},{7,6},{8,7},{9,8},{10,9},{11,1... | collective-permute-start | bytes 393224 | tf_op jit(solution)/shard_map/ppermute | solution.py:231
  82.0 5.0 %collective-permute-done.5.high_ref = bf16[256,256]{1,0:T(8,128)(2,1)S(1)} collective-permute-done((bf16[256,256]{1,0:T(8,128)(2,1)S(1)}, bf16[256,256]{1,0:T(8,128)(2,1)S(1)}, u32[]{:S(2)}, u32[]{:S(2)}) %collective-permute-start.5) | collective-permute-done | bytes 131104 | tf_op jit(solution)/shard_map/ppermute | solution.py:231
  87.0 14.5 %sublayer.3 = bf16[1024,256]{1,0:T(8,128)(2,1)} custom-call(s32[2,8]{1,0:T(2,128)S(1)} %pad_add_fusion.2.span_ref, f32[8]{0:T(128)S(1)} %get-tuple-element.32.scale_ref, s32[12,128]{1,0:T(8,128)S(1)} %get-tuple-element.23.marks_ref, s32[1,1024]{1,0:T(1,128)S(1)} %bitcast.70, bf16[256,256]{1,0:T(8,128)(2,1)S(1)} %collective-permute-done.4.low_ref, ...), custom_call_target="tpu_custom_call" | custom-call | flops 8000000000 | bytes 4000000 | tf_op jit(solution)/shard_map/sublayer/pallas_call | solution.py:147
  (31 shorter events, 0.3 us)
Async XLA Ops:
  0.7 14.0 %collective-permute-start.1 = (s32[2,256]{1,0:T(2,128)S(1)}, s32[2,256]{1,0:T(2,128)S(1)}, u32[]{:S(2)}, u32[]{:S(2)}) collective-permute-start(s32[2,256]{1,0:T(2,128)S(1)} %get-tuple-element.20), channel_id=1, source_target_pairs={{1,0},{2,1},{3,2},{4,3},{5,4},{6,5},{7,6},{8,7},{9,8},{10,9},{11,1... | collective-permute-start | bytes 6152 | tf_op jit(solution)/shard_map/ppermute | solution.py:231
  3.3 11.5 %collective-permute-start = (s32[2,256]{1,0:T(2,128)S(1)}, s32[2,256]{1,0:T(2,128)S(1)}, u32[]{:S(2)}, u32[]{:S(2)}) collective-permute-start(s32[2,256]{1,0:T(2,128)S(1)} %get-tuple-element.19), channel_id=1, source_target_pairs={{0,1},{1,2},{2,3},{3,4},{4,5},{5,6},{6,7},{7,8},{8,9},{9,10},{10,1... | collective-permute-start | bytes 6152 | tf_op jit(solution)/shard_map/ppermute | solution.py:230
  8.2 6.9 %collective-permute-start.2 = (bf16[256,256]{1,0:T(8,128)(2,1)S(1)}, bf16[256,256]{1,0:T(8,128)(2,1)S(1)}, u32[]{:S(2)}, u32[]{:S(2)}) collective-permute-start(bf16[256,256]{1,0:T(8,128)(2,1)S(1)} %get-tuple-element.14), channel_id=1, source_target_pairs={{0,1},{1,2},{2,3},{3,4},{4,5},{5,6},{6,7},{7,8},{8,9},{9,10},{10,1... | collective-permute-start | bytes 393224 | tf_op jit(solution)/shard_map/ppermute | solution.py:230
  10.1 7.2 %collective-permute-start.3 = (bf16[256,256]{1,0:T(8,128)(2,1)S(1)}, bf16[256,256]{1,0:T(8,128)(2,1)S(1)}, u32[]{:S(2)}, u32[]{:S(2)}) collective-permute-start(bf16[256,256]{1,0:T(8,128)(2,1)S(1)} %get-tuple-element.13), channel_id=1, source_target_pairs={{1,0},{2,1},{3,2},{4,3},{5,4},{6,5},{7,6},{8,7},{9,8},{10,9},{11,1... | collective-permute-start | bytes 393224 | tf_op jit(solution)/shard_map/ppermute | solution.py:231
  12.6 1.2 %copy-start.2 = (bf16[2,256,256]{2,1,0:T(8,128)(2,1)S(1)}, bf16[2,256,256]{2,1,0:T(8,128)(2,1)}, u32[]{:S(2)}) copy-start(bf16[2,256,256]{2,1,0:T(8,128)(2,1)} %param.13) | copy-start | bytes 786436
  12.6 1.3 %copy-start.3 = (f32[2,256]{1,0:T(2,128)S(1)}, f32[2,256]{1,0:T(2,128)}, u32[]{:S(2)}) copy-start(f32[2,256]{1,0:T(2,128)} %param.14) | copy-start | bytes 6148
  13.8 3.5 %copy-start = (bf16[1024,256]{1,0:T(8,128)(2,1)S(1)}, bf16[1024,256]{1,0:T(8,128)(2,1)}, u32[]{:S(2)}) copy-start(bf16[1024,256]{1,0:T(8,128)(2,1)} %hidden_ref.1) | copy-start | bytes 1572868
  13.9 0.7 copy-start.4
  17.3 0.7 copy-start.1
  32.9 41.6 %all-to-all-start = ((bf16[16,128,256]{2,1,0:T(8,128)(2,1)}), bf16[16,128,256]{2,1,0:T(8,128)(2,1)S(1)}, u32[]{:S(2)}, u32[]{:S(2)}) async-start(bf16[16,128,256]{2,1,0:T(8,128)(2,1)} %bitcast.20), calls=%async_computation | async-start | bytes 2097152 | tf_op jit(solution)/shard_map/all_to_all | solution.py:260
  75.8 6.2 %collective-permute-start.4 = (bf16[256,256]{1,0:T(8,128)(2,1)S(1)}, bf16[256,256]{1,0:T(8,128)(2,1)S(1)}, u32[]{:S(2)}, u32[]{:S(2)}) collective-permute-start(bf16[256,256]{1,0:T(8,128)(2,1)S(1)} %get-tuple-element.12), channel_id=1, source_target_pairs={{0,1},{1,2},{2,3},{3,4},{4,5},{5,6},{6,7},{7,8},{8,9},{9,10},{10,1... | collective-permute-start | bytes 393224 | tf_op jit(solution)/shard_map/ppermute | solution.py:230
  79.8 7.2 %collective-permute-start.5 = (bf16[256,256]{1,0:T(8,128)(2,1)S(1)}, bf16[256,256]{1,0:T(8,128)(2,1)S(1)}, u32[]{:S(2)}, u32[]{:S(2)}) collective-permute-start(bf16[256,256]{1,0:T(8,128)(2,1)S(1)} %get-tuple-element.11), channel_id=1, source_target_pairs={{1,0},{2,1},{3,2},{4,3},{5,4},{6,5},{7,6},{8,7},{9,8},{10,9},{11,1... | collective-permute-start | bytes 393224 | tf_op jit(solution)/shard_map/ppermute | solution.py:231

commit v2 on v1

v2 whole, which is shorter than its diff:
```python
import functools
import math

import jax
import jax.numpy as jnp
from jax import lax
from jax.experimental import pallas as pl
from jax.experimental.pallas import tpu as pltpu
from jax.sharding import PartitionSpec as P

HEADS = 8
TILE = 128
TAIL = 16

epsilon = 1e-05
masked_score = -1e30
no_mark = 1 << 30
vmem_limit = 40 * 1024 * 1024

vmem = pl.BlockSpec(memory_space=pltpu.VMEM)
smem = pl.BlockSpec(memory_space=pltpu.SMEM)


def dot(a, b):
    return jnp.dot(a, b, preferred_element_type=jnp.float32)


def dot_t(a, b):
    return lax.dot_general(a, b, (((1,), (1,)), ((), ())), preferred_element_type=jnp.float32)


def one_hot(hits):
    return jnp.where(hits, 1.0, 0.0).astype(jnp.bfloat16)


def ranks(match):
    rows, columns = match.shape
    before = one_hot(
        lax.broadcasted_iota(jnp.int32, (TILE, TILE), 0)
        < lax.broadcasted_iota(jnp.int32, (TILE, TILE), 1)
    )
    carry = jnp.zeros((rows, 1), jnp.float32)
    pieces = []
    for start in range(0, columns, TILE):
        piece = match[:, start : start + TILE]
        pieces.append(dot(piece.astype(jnp.bfloat16), before) + carry)
        carry = carry + jnp.sum(piece, axis=1, keepdims=True)
    return jnp.concatenate(pieces, axis=1)


def project_kernel(layer, hidden_ref, w_qkv_ref, query_ref, key_ref, value_ref):
    rows, channels = hidden_ref.shape
    chunk = min(256, rows)
    w_value = jnp.transpose(w_qkv_ref[layer, :, 2 * channels :])
    for start in range(0, rows, chunk):
        here = slice(start, start + chunk)
        both = dot(hidden_ref[here], w_qkv_ref[layer, :, : 2 * channels]).astype(jnp.bfloat16)
        query_ref[here] = both[:, :channels]
        key_ref[here] = both[:, channels:]
        value_ref[:, here] = dot_t(w_value, hidden_ref[here]).astype(jnp.bfloat16)


def run_project(layer, hidden, w_qkv):
    rows, channels = hidden.shape
    return pl.pallas_call(
        functools.partial(project_kernel, layer),
        out_shape=(
            jax.ShapeDtypeStruct((rows, channels), jnp.bfloat16),
            jax.ShapeDtypeStruct((rows, channels), jnp.bfloat16),
            jax.ShapeDtypeStruct((channels, rows), jnp.bfloat16),
        ),
        in_specs=[vmem, vmem],
        out_specs=(vmem, vmem, vmem),
        compiler_params=pltpu.CompilerParams(vmem_limit_bytes=vmem_limit),
        cost_estimate=pl.CostEstimate(
            flops=6 * rows * channels * channels, bytes_accessed=3 * 10**6, transcendentals=0
        ),
        name="project",
    )(hidden, w_qkv)


def attend_tile(
    number, span_ref, scales, marks_ref, column_ref, query_ref, key_ref, value_ref, attended_ref,
    rim,
):
    channels = query_ref.shape[1]
    head_dim = channels // HEADS
    per_group = TILE // head_dim
    groups = channels // TILE
    row = pl.multiple_of(number * TILE, TILE)
    low = span_ref[0, number]
    count = span_ref[1, number]
    most = 1 + 2 * (rim // TILE)
    lane_head = lax.broadcasted_iota(jnp.int32, (TILE, TILE), 1) // head_dim

    def variant(tiles):
        first_key = pl.multiple_of(low * TILE, TILE)
        span = pl.ds(first_key, tiles * TILE)
        own = marks_ref[pl.ds(number + rim // TILE, 1), :]
        bias = jnp.where(column_ref[span, :] == own, 0.0, masked_score)
        for group in range(groups):
            lanes = slice(group * TILE, (group + 1) * TILE)
            query = query_ref[pl.ds(row, TILE), lanes]
            stacked = jnp.concatenate(
                [jnp.where(lane_head == j, query, 0.0).astype(jnp.bfloat16) for j in range(per_group)],
                axis=0,
            )
            scores = dot_t(key_ref[span, lanes], stacked)
            for pair in range(0, per_group, 2):
                weights = []
                for j in (pair, pair + 1):
                    part = scores[:, j * TILE : (j + 1) * TILE] * scales[group * per_group + j]
                    part = part + bias
                    part = jnp.exp2(part - jnp.max(part, axis=0, keepdims=True))
                    part = part * (1.0 / jnp.sum(part, axis=0, keepdims=True))
                    weights.append(part.astype(jnp.bfloat16))
                begin = group * TILE + pair * head_dim
                mixed = dot(
                    value_ref[begin : begin + 2 * head_dim, span], jnp.concatenate(weights, axis=1)
                )
                attended_ref[pl.ds(number, 1), begin : begin + head_dim] = mixed[:head_dim, :TILE][None]
                attended_ref[pl.ds(number, 1), begin + head_dim : begin + 2 * head_dim] = mixed[
                    head_dim:, TILE:
                ][None]

    for tiles in range(2, most + 1):
        pl.when(jnp.maximum(count, 2) == tiles)(functools.partial(variant, tiles))


def halo_marks(tail_ref, layer, rim):
    channels = tail_ref.shape[1]
    found = []
    for start in range(0, rim, TILE):
        digits = []
        for digit in range(2):
            place = (2 * layer + digit) * rim + start
            line, lane = rim + place // channels, place % channels
            digits.append(tail_ref[rim : rim + TAIL, lane : lane + TILE].astype(jnp.float32)[line - rim : line - rim + 1])
        found.append((digits[0] * 256.0 + digits[1]).astype(jnp.int32))
    return found


def sublayer_kernel(
    layer, packing, temper_ref, window_ref, dest_ref, marks_own_ref, low_tail_ref, high_tail_ref,
    low_ref, hidden_ref, high_ref, query_ref, key_own_ref, value_own_ref, w_qkv_ref, w_out_ref,
    gain_ref, out_ref, span_ref, marks_ref, column_ref, key_ref, value_ref, attended_ref, first_ref,
):
    rows, channels = hidden_ref.shape
    rim = rows // 4
    rim_tiles, own_tiles = rim // TILE, rows // TILE
    factor = (1.0 / math.sqrt(channels // HEADS)) * math.log2(math.e)
    scales = [temper_ref[layer, j] * factor for j in range(HEADS)]

    low_marks = halo_marks(low_tail_ref, layer, rim)
    high_marks = [jnp.where(m == 0, no_mark, m) for m in halo_marks(high_tail_ref, layer, rim)]
    for i in range(rim_tiles):
        marks_ref[i : i + 1] = low_marks[i]
        marks_ref[rim_tiles + own_tiles + i : rim_tiles + own_tiles + i + 1] = high_marks[i]
    marks_ref[rim_tiles : rim_tiles + own_tiles] = marks_own_ref[...] + 1
    lasts = [jnp.max(m) for m in low_marks]
    firsts = [jnp.min(m) for m in high_marks]
    own_first = [window_ref[i * TILE] + 1 for i in range(own_tiles)]
    own_last = [window_ref[(i + 1) * TILE - 1] + 1 for i in range(own_tiles)]
    for t in range(own_tiles):
        begin = jnp.int32(0)
        for mark in lasts + own_last[:t]:
            begin += (mark < own_first[t]).astype(jnp.int32)
        end = jnp.int32(rim_tiles + t + 1)
        for mark in own_first[t + 1 :] + firsts:
            end += (mark <= own_last[t]).astype(jnp.int32)
        span_ref[0, t] = begin
        span_ref[1, t] = end - begin
    for i in range(2 * rim_tiles + own_tiles):
        column_ref[i * TILE : (i + 1) * TILE] = jnp.transpose(
            jnp.broadcast_to(marks_ref[i : i + 1, :], (TILE, TILE))
        )

    w_value = jnp.transpose(w_qkv_ref[layer, :, 2 * channels :])
    key_ref[rim : rim + rows] = key_own_ref[...]
    value_ref[:, rim : rim + rows] = value_own_ref[...]
    for source, start in ((low_ref, 0), (high_ref, rim + rows)):
        source = source[:rim]
        key_ref[start : start + rim] = dot(
            source, w_qkv_ref[layer, :, channels : 2 * channels]
        ).astype(jnp.bfloat16)
        value_ref[:, start : start + rim] = dot_t(w_value, source).astype(jnp.bfloat16)

    def one_tile(number, nothing):
        attend_tile(
            number, span_ref, scales, marks_ref, column_ref, query_ref, key_ref, value_ref,
            attended_ref, rim,
        )
        return nothing

    lax.fori_loop(0, own_tiles, one_tile, 0)
    final_ref = first_ref if packing else out_ref
    for number in range(own_tiles):
        here = slice(number * TILE, (number + 1) * TILE)
        attended = jnp.transpose(attended_ref[number]).astype(jnp.bfloat16)
        summed = hidden_ref[here].astype(jnp.float32) + dot(attended, w_out_ref[layer])
        center = jnp.mean(summed, axis=1, keepdims=True)
        summed = summed - center
        spread = jnp.mean(jnp.square(summed), axis=1, keepdims=True)
        scaled = summed * lax.rsqrt(spread + epsilon) * gain_ref[layer : layer + 1]
        final_ref[here] = scaled.astype(jnp.bfloat16)
    if packing:
        pack(packing, dest_ref, first_ref, out_ref)


def pack(devices, dest_ref, first_ref, out_ref):
    rows, channels = first_ref.shape
    capacity = 2 * rows // devices
    dest = jnp.concatenate([dest_ref[i : i + 1] for i in range(rows // TILE)], axis=1)
    target = dest // rows
    match = jnp.where(lax.broadcasted_iota(jnp.int32, (devices, rows), 0) == target, 1.0, 0.0)
    place = jnp.sum(ranks(match) * match, axis=0, keepdims=True).astype(jnp.int32)
    place = place + target * capacity
    slot = dest - target * rows
    which = lax.broadcasted_iota(jnp.int32, (TAIL, rows), 0)
    digits = jnp.where(
        which == 0, slot // 32 + 1, jnp.where(which == 1, slot % 32, 0)
    )
    digits = digits.astype(jnp.float32).astype(jnp.bfloat16)
    together = max(1, 512 // capacity)
    index = lax.broadcasted_iota(jnp.int32, (together * capacity, rows), 0)
    for start in range(0, devices, together):
        hits = one_hot(index == place - start * capacity)
        packed = dot(hits, first_ref[...]).astype(jnp.bfloat16)
        slots = dot_t(digits, hits)
        for i in range(together):
            here = slice(i * capacity, (i + 1) * capacity)
            out_ref[start + i, :capacity] = packed[here]
            mine = slots[:, here]
            if capacity < TILE:
                blank = jnp.zeros((TAIL, TILE - capacity), jnp.float32)
                mine = jnp.concatenate([mine, blank], axis=1)
            extra = jnp.concatenate([mine[0:8], pltpu.roll(mine[0:8], 7, 0)], axis=1)
            out_ref[start + i, capacity:] = extra.astype(jnp.bfloat16)


def run_sublayer(layer, packing, temper, window, dest, tails, low, hidden, high, w_qkv, w_out, gain):
    rows, channels = hidden.shape
    rim = rows // 4
    tiles = rows // TILE
    seen = rows + 2 * rim
    projected = run_project(layer, hidden, w_qkv)
    shape = (packing, 2 * rows // packing + 8, channels) if packing else (rows, channels)
    return pl.pallas_call(
        functools.partial(sublayer_kernel, layer, packing),
        out_shape=jax.ShapeDtypeStruct(shape, jnp.bfloat16),
        in_specs=[smem, smem] + [vmem] * 13,
        out_specs=vmem,
        scratch_shapes=[
            pltpu.SMEM((2, tiles), jnp.int32),
            pltpu.VMEM((seen // TILE, TILE), jnp.int32),
            pltpu.VMEM((seen, TILE), jnp.int32),
            pltpu.VMEM((seen, channels), jnp.bfloat16),
            pltpu.VMEM((channels, seen), jnp.bfloat16),
            pltpu.VMEM((tiles, channels, TILE), jnp.float32),
            pltpu.VMEM((rows, channels), jnp.bfloat16),
        ],
        compiler_params=pltpu.CompilerParams(vmem_limit_bytes=vmem_limit),
        cost_estimate=pl.CostEstimate(
            flops=8 * 10**9, bytes_accessed=4 * 10**6, transcendentals=8 * 10**6
        ),
        name="sublayer",
    )(
        temper, window, dest.reshape(tiles, TILE), window.reshape(tiles, TILE), *tails, low, hidden,
        high, *projected, w_qkv, w_out, gain,
    )


def place_kernel(arrived_ref, moved_ref):
    rows = moved_ref.shape[0]
    devices, padded, channels = arrived_ref.shape
    capacity = padded - 8
    slots = []
    for i in range(devices):
        line = arrived_ref[i, capacity:].astype(jnp.float32)
        value = line[0:1, :capacity] * 32.0 + line[0:1, TILE : TILE + capacity] - 32.0
        slots.append(value.astype(jnp.int32))
    arrived = jnp.concatenate([arrived_ref[i, :capacity] for i in range(devices)], axis=0)
    chunk = min(256, rows)
    for start in range(0, rows, chunk):
        index = lax.broadcasted_iota(jnp.int32, (chunk, capacity), 0) + start
        hits = jnp.concatenate([one_hot(index == slots[i]) for i in range(devices)], axis=1)
        moved_ref[start : start + chunk] = dot(hits, arrived).astype(jnp.bfloat16)


def run_place(arrived, rows):
    return pl.pallas_call(
        place_kernel,
        out_shape=jax.ShapeDtypeStruct((rows, arrived.shape[2]), jnp.bfloat16),
        in_specs=[vmem],
        out_specs=vmem,
        compiler_params=pltpu.CompilerParams(vmem_limit_bytes=vmem_limit),
        cost_estimate=pl.CostEstimate(
            flops=10**9, bytes_accessed=2 * 10**6, transcendentals=0
        ),
        name="place",
    )(arrived)


def exchange(to_right, to_left):
    count = lax.axis_size("wide")
    forward = [(i, i + 1) for i in range(count - 1)]
    backward = [(target, source) for source, target in forward]
    return lax.ppermute(to_right, "wide", forward), lax.ppermute(to_left, "wide", backward)


def with_marks(features, windows):
    channels = features.shape[1]
    marks = windows + 1
    digits = jnp.stack([marks // 256, marks % 256], axis=1).reshape(-1)
    digits = jnp.pad(digits, (0, TAIL * channels - digits.shape[0])).reshape(TAIL, channels)
    return jnp.concatenate([features, digits.astype(jnp.bfloat16)], axis=0)


def body(voxels, regular_window, shifted_window, dest, w_qkv, w_out, gain, temper):
    rows, channels = voxels.shape
    rim = rows // 4
    devices = lax.axis_size("wide")
    windows = jnp.stack([regular_window, shifted_window])
    tails = exchange(
        with_marks(voxels[rows - rim :], windows[:, rows - rim :]),
        with_marks(voxels[:rim], windows[:, :rim]),
    )
    outgoing = run_sublayer(
        0, devices, temper, regular_window, dest, tails, tails[0], voxels, tails[1], w_qkv, w_out,
        gain,
    )
    arrived = lax.all_to_all(outgoing, "wide", split_axis=0, concat_axis=0, tiled=True)
    moved = run_place(arrived, rows)
    low, high = exchange(moved[rows - rim :], moved[:rim])
    return run_sublayer(
        1, 0, temper, shifted_window, dest, tails, low, moved, high, w_qkv, w_out, gain
    )


def solution(mesh):
    in_specs = (
        P(("parts", "wide"), None),
        P(("parts", "wide")),
        P(("parts", "wide")),
        P(("parts", "wide")),
        P(),
        P(),
        P(),
        P(),
    )
    out_specs = P(("parts", "wide"), None)
    return jax.shard_map(body, mesh=mesh, in_specs=in_specs, out_specs=out_specs, check_vma=False)
```

time: 102 us -> 82.6 us (0.81)
  the two profiles are of different devices: /device:TPU:13 before, /device:TPU:8 now
where the time goes in v2:
time: 82.6 us; the launch traced here: 82.2 us
  blocking collectives  33.3 us (40%)
  Pallas kernels  28.5 us (35%)
  starting transfers between devices  11.7 us (14%)
  waiting for transfers between devices  5.3 us (6%)
  local copies, waits for them, and re-layouts  2.23 us (3%)
  other arithmetic  0.87 us (1%)
    all_to_all x1, blocking collectives, body(): lax.all_to_all(outgoing, 'wide', split_axis=0, concat_axis=0, tiled=True)  33.3 us
    pallas_call x2, Pallas kernels, run_sublayer(): pl.pallas_call(functools.partial(sublayer_kernel, layer, packing), out_sh...  26.1 us
    ppermute x2, starting transfers between devices, exchange(): lax.ppermute(to_left, 'wide', backward)  7.59 us
    ppermute x2, waiting for transfers between devices, exchange(): lax.ppermute(to_right, 'wide', forward)  4.47 us
    ppermute x2, starting transfers between devices, exchange(): lax.ppermute(to_right, 'wide', forward)  4.15 us
  transfers between devices with their start and end apart: 4, of which 2 were waited for; matrix products, arithmetic and copies ran while one was open for 0% of the time, Pallas kernels for 1%

profile of v2, /device:TPU:8, one launch (start us, length us, event | category | flops | bytes accessed | tf_op | source)
XLA Modules:
  0.0 82.2 jit_solution(8628144202784483672)
XLA Ops:
  0.0 0.8 fusion.7
  0.9 1.0 %fusion.11 = (bf16[256,256]{1,0:T(8,128)(2,1)S(1)}, bf16[256,256]{1,0:T(8,128)(2,1)S(1)}) fusion(bf16[1024,256]{1,0:T(8,128)(2,1)} %hidden_ref.3), kind=kLoop, calls=%fused_computation.32 | loop fusion | bytes 524288 | tf_op jit(solution)/shard_map/slice | solution.py:326
  1.9 0.0 copy-start.1
  1.9 0.0 copy-start.5
  1.9 0.0 copy-start.6
  1.9 0.0 copy-start.7
  2.0 0.0 copy-start.8
  2.0 2.1 %collective-permute-start = (bf16[272,256]{1,0:T(8,128)(2,1)S(1)}, bf16[272,256]{1,0:T(8,128)(2,1)S(1)}, u32[]{:S(2)}, u32[]{:S(2)}) collective-permute-start(bf16[272,256]{1,0:T(8,128)(2,1)S(1)} %pad_maximum_fusion), channel_id=1, source_target_pairs={{0,1},{1,2},{2,3},{3,4},{4,5},{5,6},{6,7},{7,8},{8,9},{9,10},{10,1... | collective-permute-start | bytes 417800 | tf_op jit(solution)/shard_map/ppermute | solution.py:308
  4.1 4.5 %collective-permute-start.1 = (bf16[272,256]{1,0:T(8,128)(2,1)S(1)}, bf16[272,256]{1,0:T(8,128)(2,1)S(1)}, u32[]{:S(2)}, u32[]{:S(2)}) collective-permute-start(bf16[272,256]{1,0:T(8,128)(2,1)S(1)} %pad_maximum_fusion.1), channel_id=1, source_target_pairs={{1,0},{2,1},{3,2},{4,3},{5,4},{6,5},{7,6},{8,7},{9,8},{10,9},{11,1... | collective-permute-start | bytes 417800 | tf_op jit(solution)/shard_map/ppermute | solution.py:308
  8.7 0.0 copy-start.3
  8.7 1.1 %copy-done.3 = bf16[2,256,768]{2,1,0:T(8,128)(2,1)S(1)} copy-done((bf16[2,256,768]{2,1,0:T(8,128)(2,1)S(1)}, bf16[2,256,768]{2,1,0:T(8,128)(2,1)}, u32[]{:S(2)}) %copy-start.3) | copy-done | bytes 786456
  9.8 0.6 project.2
  10.4 0.0 collective-permute-done.low_tail_ref.low_ref
  10.4 0.8 %collective-permute-done.1.high_tail_ref.high_ref = bf16[272,256]{1,0:T(8,128)(2,1)S(1)} collective-permute-done((bf16[272,256]{1,0:T(8,128)(2,1)S(1)}, bf16[272,256]{1,0:T(8,128)(2,1)S(1)}, u32[]{:S(2)}, u32[]{:S(2)}) %collective-permute-start.1) | collective-permute-done | bytes 139296 | tf_op jit(solution)/shard_map/ppermute | solution.py:308
  11.3 13.7 %sublayer.2 = bf16[16,136,256]{2,1,0:T(8,128)(2,1)S(1)} custom-call(f32[2,8]{1,0:T(2,128)S(1)} %copy-done.8, s32[1024]{0:T(1024)S(1)} %copy-done.1, s32[8,128]{1,0:T(8,128)S(1)} %bitcast.25, s32[8,128]{1,0:T(8,128)S(1)} %bitcast.22, bf16[272,256]{1,0:T(8,128)(2,1)S(1)} %collective-permute-done.low_tail_ref.low_ref, ...), custom_call_target="tpu_custom_call" | custom-call | flops 8000000000 | bytes 4000000 | tf_op jit(solution)/shard_map/sublayer/pallas_call | solution.py:248
  24.9 33.3 %all_to_all.5.arrived_ref = bf16[16,136,256]{2,1,0:T(8,128)(2,1)S(1)} all-to-all(bf16[16,136,256]{2,1,0:T(8,128)(2,1)S(1)} %sublayer.2), channel_id=1, replica_groups=mesh['parts'=2,'wide'=16] {'wide'}, dimensions={0} | all-to-all | bytes 2228224 | tf_op jit(solution)/shard_map/all_to_all | solution.py:332
  58.2 1.2 %place.1.hidden_ref = bf16[1024,256]{1,0:T(8,128)(2,1)S(1)} custom-call(bf16[16,136,256]{2,1,0:T(8,128)(2,1)S(1)} %all_to_all.5.arrived_ref), custom_call_target="tpu_custom_call" | custom-call | flops 1000000000 | bytes 2000000 | tf_op jit(solution)/shard_map/place/pallas_call | solution.py:291
  59.5 0.0 copy-start.2
  59.5 3.0 %collective-permute-start.3 = (bf16[256,256]{1,0:T(8,128)(2,1)S(1)}, bf16[256,256]{1,0:T(8,128)(2,1)S(1)}, u32[]{:S(2)}, u32[]{:S(2)}) collective-permute-start(bf16[256,256]{1,0:T(8,128)(2,1)S(1)} %get-tuple-element.21), channel_id=1, source_target_pairs={{1,0},{2,1},{3,2},{4,3},{5,4},{6,5},{7,6},{8,7},{9,8},{10,9},{11,1... | collective-permute-start | bytes 393224 | tf_op jit(solution)/shard_map/ppermute | solution.py:308
  62.6 2.1 %collective-permute-start.2 = (bf16[256,256]{1,0:T(8,128)(2,1)S(1)}, bf16[256,256]{1,0:T(8,128)(2,1)S(1)}, u32[]{:S(2)}, u32[]{:S(2)}) collective-permute-start(bf16[256,256]{1,0:T(8,128)(2,1)S(1)} %get-tuple-element.22), channel_id=1, source_target_pairs={{0,1},{1,2},{2,3},{3,4},{4,5},{5,6},{6,7},{7,8},{8,9},{9,10},{10,1... | collective-permute-start | bytes 393224 | tf_op jit(solution)/shard_map/ppermute | solution.py:308
  64.7 0.6 project.3
  65.3 0.0 collective-permute-done.3.high_ref
  65.3 4.5 %collective-permute-done.2.low_ref = bf16[256,256]{1,0:T(8,128)(2,1)S(1)} collective-permute-done((bf16[256,256]{1,0:T(8,128)(2,1)S(1)}, bf16[256,256]{1,0:T(8,128)(2,1)S(1)}, u32[]{:S(2)}, u32[]{:S(2)}) %collective-permute-start.2) | collective-permute-done | bytes 131104 | tf_op jit(solution)/shard_map/ppermute | solution.py:308
  69.8 12.5 %sublayer.3 = bf16[1024,256]{1,0:T(8,128)(2,1)} custom-call(f32[2,8]{1,0:T(2,128)S(1)} %copy-done.8, s32[1024]{0:T(1024)S(1)} %copy-done.2, s32[8,128]{1,0:T(8,128)S(1)} %bitcast.26, s32[8,128]{1,0:T(8,128)S(1)} %bitcast.24, bf16[272,256]{1,0:T(8,128)(2,1)S(1)} %collective-permute-done.low_tail_ref.low_ref, ...), custom_call_target="tpu_custom_call" | custom-call | flops 8000000000 | bytes 4000000 | tf_op jit(solution)/shard_map/sublayer/pallas_call | solution.py:248
  (24 shorter events, 0.1 us)
Async XLA Ops:
  0.0 8.7 %copy-start = (bf16[1024,256]{1,0:T(8,128)(2,1)S(1)}, bf16[1024,256]{1,0:T(8,128)(2,1)}, u32[]{:S(2)}) copy-start(bf16[1024,256]{1,0:T(8,128)(2,1)} %hidden_ref.3) | copy-start | bytes 1572868
  1.9 9.3 %copy-start.1 = (s32[1024]{0:T(1024)S(1)}, s32[1024]{0:T(1024)}, u32[]{:S(2)}) copy-start(s32[1024]{0:T(1024)} %window_ref.2) | copy-start | bytes 12292
  1.9 9.3 %copy-start.5 = (bf16[2,256,256]{2,1,0:T(8,128)(2,1)S(1)}, bf16[2,256,256]{2,1,0:T(8,128)(2,1)}, u32[]{:S(2)}) copy-start(bf16[2,256,256]{2,1,0:T(8,128)(2,1)} %w_out_ref.3) | copy-start | bytes 786436
  1.9 9.3 %copy-start.6 = (s32[1024]{0:T(1024)S(1)}, s32[1024]{0:T(1024)}, u32[]{:S(2)}) copy-start(s32[1024]{0:T(1024)} %param.11) | copy-start | bytes 12292
  1.9 9.3 %copy-start.7 = (f32[2,256]{1,0:T(2,128)S(1)}, f32[2,256]{1,0:T(2,128)}, u32[]{:S(2)}) copy-start(f32[2,256]{1,0:T(2,128)} %gain_ref.3) | copy-start | bytes 6148
  2.0 9.3 %copy-start.8 = (f32[2,8]{1,0:T(2,128)S(1)}, f32[2,8]{1,0:T(2,128)}, u32[]{:S(2)}) copy-start(f32[2,8]{1,0:T(2,128)} %temper_ref.3) | copy-start | bytes 196
  2.0 8.4 %collective-permute-start = (bf16[272,256]{1,0:T(8,128)(2,1)S(1)}, bf16[272,256]{1,0:T(8,128)(2,1)S(1)}, u32[]{:S(2)}, u32[]{:S(2)}) collective-permute-start(bf16[272,256]{1,0:T(8,128)(2,1)S(1)} %pad_maximum_fusion), channel_id=1, source_target_pairs={{0,1},{1,2},{2,3},{3,4},{4,5},{5,6},{6,7},{7,8},{8,9},{9,10},{10,1... | collective-permute-start | bytes 417800 | tf_op jit(solution)/shard_map/ppermute | solution.py:308
  4.1 7.1 %collective-permute-start.1 = (bf16[272,256]{1,0:T(8,128)(2,1)S(1)}, bf16[272,256]{1,0:T(8,128)(2,1)S(1)}, u32[]{:S(2)}, u32[]{:S(2)}) collective-permute-start(bf16[272,256]{1,0:T(8,128)(2,1)S(1)} %pad_maximum_fusion.1), channel_id=1, source_target_pairs={{1,0},{2,1},{3,2},{4,3},{5,4},{6,5},{7,6},{8,7},{9,8},{10,9},{11,1... | collective-permute-start | bytes 417800 | tf_op jit(solution)/shard_map/ppermute | solution.py:308
  8.7 1.1 %copy-start.3 = (bf16[2,256,768]{2,1,0:T(8,128)(2,1)S(1)}, bf16[2,256,768]{2,1,0:T(8,128)(2,1)}, u32[]{:S(2)}) copy-start(bf16[2,256,768]{2,1,0:T(8,128)(2,1)} %w_qkv_ref.7) | copy-start | bytes 2359300
  58.2 6.5 %copy-start.4 = (bf16[2,256,768]{2,1,0:T(8,128)(2,1)S(1)}, bf16[2,256,768]{2,1,0:T(8,128)(2,1)}, u32[]{:S(2)}) copy-start(bf16[2,256,768]{2,1,0:T(8,128)(2,1)} %w_qkv_ref.7) | copy-start | bytes 2359300
  59.5 10.3 %copy-start.2 = (s32[1024]{0:T(1024)S(1)}, s32[1024]{0:T(1024)}, u32[]{:S(2)}) copy-start(s32[1024]{0:T(1024)} %window_ref.3) | copy-start | bytes 12292
  59.5 5.8 %collective-permute-start.3 = (bf16[256,256]{1,0:T(8,128)(2,1)S(1)}, bf16[256,256]{1,0:T(8,128)(2,1)S(1)}, u32[]{:S(2)}, u32[]{:S(2)}) collective-permute-start(bf16[256,256]{1,0:T(8,128)(2,1)S(1)} %get-tuple-element.21), channel_id=1, source_target_pairs={{1,0},{2,1},{3,2},{4,3},{5,4},{6,5},{7,6},{8,7},{9,8},{10,9},{11,1... | collective-permute-start | bytes 393224 | tf_op jit(solution)/shard_map/ppermute | solution.py:308
  62.6 7.2 %collective-permute-start.2 = (bf16[256,256]{1,0:T(8,128)(2,1)S(1)}, bf16[256,256]{1,0:T(8,128)(2,1)S(1)}, u32[]{:S(2)}, u32[]{:S(2)}) collective-permute-start(bf16[256,256]{1,0:T(8,128)(2,1)S(1)} %get-tuple-element.22), channel_id=1, source_target_pairs={{0,1},{1,2},{2,3},{3,4},{4,5},{5,6},{6,7},{7,8},{8,9},{9,10},{10,1... | collective-permute-start | bytes 393224 | tf_op jit(solution)/shard_map/ppermute | solution.py:308

commit v3 on v2

--- a/solution.py
+++ b/solution.py
@@ -51,13 +51,18 @@
 def project_kernel(layer, hidden_ref, w_qkv_ref, query_ref, key_ref, value_ref):
     rows, channels = hidden_ref.shape
     chunk = min(256, rows)
+    w_query = jnp.transpose(w_qkv_ref[layer, :, :channels])
     w_value = jnp.transpose(w_qkv_ref[layer, :, 2 * channels :])
+    w_both = jnp.concatenate([w_query, w_value], axis=0)
     for start in range(0, rows, chunk):
         here = slice(start, start + chunk)
-        both = dot(hidden_ref[here], w_qkv_ref[layer, :, : 2 * channels]).astype(jnp.bfloat16)
-        query_ref[here] = both[:, :channels]
-        key_ref[here] = both[:, channels:]
-        value_ref[:, here] = dot_t(w_value, hidden_ref[here]).astype(jnp.bfloat16)
+        source = hidden_ref[here]
+        key_ref[here] = dot(source, w_qkv_ref[layer, :, channels : 2 * channels]).astype(
+            jnp.bfloat16
+        )
+        both = dot_t(w_both, source).astype(jnp.bfloat16)
+        query_ref[:, here] = both[:channels]
+        value_ref[:, here] = both[channels:]
 
 
 def run_project(layer, hidden, w_qkv):
@@ -65,7 +70,7 @@
     return pl.pallas_call(
         functools.partial(project_kernel, layer),
         out_shape=(
-            jax.ShapeDtypeStruct((rows, channels), jnp.bfloat16),
+            jax.ShapeDtypeStruct((channels, rows), jnp.bfloat16),
             jax.ShapeDtypeStruct((rows, channels), jnp.bfloat16),
             jax.ShapeDtypeStruct((channels, rows), jnp.bfloat16),
         ),
@@ -83,7 +88,7 @@
     number, span_ref, scales, marks_ref, column_ref, query_ref, key_ref, value_ref, attended_ref,
     rim,
 ):
-    channels = query_ref.shape[1]
+    channels = query_ref.shape[0]
     head_dim = channels // HEADS
     per_group = TILE // head_dim
     groups = channels // TILE
@@ -91,58 +96,90 @@
     low = span_ref[0, number]
     count = span_ref[1, number]
     most = 1 + 2 * (rim // TILE)
-    lane_head = lax.broadcasted_iota(jnp.int32, (TILE, TILE), 1) // head_dim
+    blank = jnp.zeros((head_dim, TILE), jnp.bfloat16)
 
     def variant(tiles):
         first_key = pl.multiple_of(low * TILE, TILE)
         span = pl.ds(first_key, tiles * TILE)
         own = marks_ref[pl.ds(number + rim // TILE, 1), :]
         bias = jnp.where(column_ref[span, :] == own, 0.0, masked_score)
-        for group in range(groups):
-            lanes = slice(group * TILE, (group + 1) * TILE)
-            query = query_ref[pl.ds(row, TILE), lanes]
-            stacked = jnp.concatenate(
-                [jnp.where(lane_head == j, query, 0.0).astype(jnp.bfloat16) for j in range(per_group)],
-                axis=0,
-            )
-            scores = dot_t(key_ref[span, lanes], stacked)
-            for pair in range(0, per_group, 2):
-                weights = []
-                for j in (pair, pair + 1):
-                    part = scores[:, j * TILE : (j + 1) * TILE] * scales[group * per_group + j]
-                    part = part + bias
-                    part = jnp.exp2(part - jnp.max(part, axis=0, keepdims=True))
-                    part = part * (1.0 / jnp.sum(part, axis=0, keepdims=True))
-                    weights.append(part.astype(jnp.bfloat16))
-                begin = group * TILE + pair * head_dim
-                mixed = dot(
-                    value_ref[begin : begin + 2 * head_dim, span], jnp.concatenate(weights, axis=1)
-                )
-                attended_ref[pl.ds(number, 1), begin : begin + head_dim] = mixed[:head_dim, :TILE][None]
-                attended_ref[pl.ds(number, 1), begin + head_dim : begin + 2 * head_dim] = mixed[
-                    head_dim:, TILE:
-                ][None]
+        parts = []
+        for j in range(HEADS):
+            group = j * head_dim // TILE
+            column = [blank] * per_group
+            column[j % per_group] = query_ref[j * head_dim : (j + 1) * head_dim, pl.ds(row, TILE)]
+            keys = key_ref[span, group * TILE : (group + 1) * TILE]
+            parts.append(dot(keys, jnp.concatenate(column, axis=0)))
+        weights = []
+        for j in range(HEADS):
+            part = parts[j] * scales[j] + bias
+            part = jnp.exp2(part - jnp.max(part, axis=0, keepdims=True))
+            part = part * (1.0 / jnp.sum(part, axis=0, keepdims=True))
+            weights.append(part.astype(jnp.bfloat16))
+        for j in range(HEADS):
+            begin = j * head_dim
+            mixed = dot(value_ref[begin : begin + head_dim, span], weights[j])
+            attended_ref[pl.ds(number, 1), begin : begin + head_dim] = mixed[None]
 
     for tiles in range(2, most + 1):
         pl.when(jnp.maximum(count, 2) == tiles)(functools.partial(variant, tiles))
 
 
-def halo_marks(tail_ref, layer, rim):
-    channels = tail_ref.shape[1]
+def mark_place(layer, digit, start, rim, channels):
+    place = (2 * layer + digit) * rim + start
+    return place // channels, place % channels
+
+
+def halo_marks(tail, layer, rim):
     found = []
     for start in range(0, rim, TILE):
         digits = []
         for digit in range(2):
-            place = (2 * layer + digit) * rim + start
-            line, lane = rim + place // channels, place % channels
-            digits.append(tail_ref[rim : rim + TAIL, lane : lane + TILE].astype(jnp.float32)[line - rim : line - rim + 1])
+            line, lane = mark_place(layer, digit, start, rim, tail.shape[1])
+            digits.append(tail[line : line + 1, lane : lane + TILE])
         found.append((digits[0] * 256.0 + digits[1]).astype(jnp.int32))
     return found
 
 
+def tail_of(windows_refs, first_tile, rim, channels):
+    which = lax.broadcasted_iota(jnp.int32, (TAIL, TILE), 0)
+    columns = [jnp.zeros((TAIL, TILE), jnp.float32) for _ in range(channels // TILE)]
+    for layer, window_ref in enumerate(windows_refs):
+        for start in range(0, rim, TILE):
+            mark = window_ref[pl.ds(first_tile + start // TILE, 1), :] + 1
+            for digit, value in enumerate((mark // 256, mark % 256)):
+                line, lane = mark_place(layer, digit, start, rim, channels)
+                column = columns[lane // TILE]
+                columns[lane // TILE] = jnp.where(which == line, value.astype(jnp.float32), column)
+    return jnp.concatenate(columns, axis=1).astype(jnp.bfloat16)
+
+
+def edges_kernel(odd_ref, hidden_ref, regular_ref, shifted_ref, near_ref, far_ref):
+    rows, channels = hidden_ref.shape
+    rim = rows // 4
+    for out_ref, at_end in ((near_ref, 1 - odd_ref[0]), (far_ref, odd_ref[0])):
+        start = pl.multiple_of(at_end * (rows - rim), TILE)
+        out_ref[:rim] = hidden_ref[pl.ds(start, rim)]
+        out_ref[rim:] = tail_of(
+            (regular_ref, shifted_ref), at_end * ((rows - rim) // TILE), rim, channels
+        )
+
+
+def run_edges(odd, hidden, regular, shifted):
+    rows, channels = hidden.shape
+    shape = jax.ShapeDtypeStruct((rows // 4 + TAIL, channels), jnp.bfloat16)
+    return pl.pallas_call(
+        edges_kernel,
+        out_shape=(shape, shape),
+        in_specs=[smem, vmem, vmem, vmem],
+        out_specs=(vmem, vmem),
+        name="edges",
+    )(odd, hidden, regular.reshape(-1, TILE), shifted.reshape(-1, TILE))
+
+
 def sublayer_kernel(
-    layer, packing, temper_ref, window_ref, dest_ref, marks_own_ref, low_tail_ref, high_tail_ref,
-    low_ref, hidden_ref, high_ref, query_ref, key_own_ref, value_own_ref, w_qkv_ref, w_out_ref,
+    layer, packing, odd_ref, temper_ref, window_ref, dest_ref, marks_own_ref, near_tail_ref,
+    far_tail_ref, near_ref, hidden_ref, far_ref, query_ref, key_own_ref, value_own_ref, w_qkv_ref, w_out_ref,
     gain_ref, out_ref, span_ref, marks_ref, column_ref, key_ref, value_ref, attended_ref, first_ref,
 ):
     rows, channels = hidden_ref.shape
@@ -151,8 +188,13 @@
     factor = (1.0 / math.sqrt(channels // HEADS)) * math.log2(math.e)
     scales = [temper_ref[layer, j] * factor for j in range(HEADS)]
 
-    low_marks = halo_marks(low_tail_ref, layer, rim)
-    high_marks = [jnp.where(m == 0, no_mark, m) for m in halo_marks(high_tail_ref, layer, rim)]
+    odd = odd_ref[0]
+    near_tail = near_tail_ref[rim : rim + TAIL].astype(jnp.float32)
+    far_tail = far_tail_ref[rim : rim + TAIL].astype(jnp.float32)
+    is_odd = jnp.full(near_tail.shape, odd, jnp.int32) == 1
+    low_marks = halo_marks(jnp.where(is_odd, near_tail, far_tail), layer, rim)
+    high_marks = halo_marks(jnp.where(is_odd, far_tail, near_tail), layer, rim)
+    high_marks = [jnp.where(m == 0, no_mark, m) for m in high_marks]
     for i in range(rim_tiles):
         marks_ref[i : i + 1] = low_marks[i]
         marks_ref[rim_tiles + own_tiles + i : rim_tiles + own_tiles + i + 1] = high_marks[i]
@@ -178,12 +220,13 @@
     w_value = jnp.transpose(w_qkv_ref[layer, :, 2 * channels :])
     key_ref[rim : rim + rows] = key_own_ref[...]
     value_ref[:, rim : rim + rows] = value_own_ref[...]
-    for source, start in ((low_ref, 0), (high_ref, rim + rows)):
+    for source, at_end in ((near_ref, 1 - odd), (far_ref, odd)):
         source = source[:rim]
-        key_ref[start : start + rim] = dot(
-            source, w_qkv_ref[layer, :, channels : 2 * channels]
-        ).astype(jnp.bfloat16)
-        value_ref[:, start : start + rim] = dot_t(w_value, source).astype(jnp.bfloat16)
+        there = pl.ds(pl.multiple_of(at_end * (rim + rows), TILE), rim)
+        key_ref[there] = dot(source, w_qkv_ref[layer, :, channels : 2 * channels]).astype(
+            jnp.bfloat16
+        )
+        value_ref[:, there] = dot_t(w_value, source).astype(jnp.bfloat16)
 
     def one_tile(number, nothing):
         attend_tile(
@@ -238,7 +281,9 @@
             out_ref[start + i, capacity:] = extra.astype(jnp.bfloat16)
 
 
-def run_sublayer(layer, packing, temper, window, dest, tails, low, hidden, high, w_qkv, w_out, gain):
+def run_sublayer(
+    layer, packing, odd, temper, window, dest, tails, near, hidden, far, w_qkv, w_out, gain
+):
     rows, channels = hidden.shape
     rim = rows // 4
     tiles = rows // TILE
@@ -248,7 +293,7 @@
     return pl.pallas_call(
         functools.partial(sublayer_kernel, layer, packing),
         out_shape=jax.ShapeDtypeStruct(shape, jnp.bfloat16),
-        in_specs=[smem, smem] + [vmem] * 13,
+        in_specs=[smem] * 3 + [vmem] * 13,
         out_specs=vmem,
         scratch_shapes=[
             pltpu.SMEM((2, tiles), jnp.int32),
@@ -265,13 +310,14 @@
         ),
         name="sublayer",
     )(
-        temper, window, dest.reshape(tiles, TILE), window.reshape(tiles, TILE), *tails, low, hidden,
-        high, *projected, w_qkv, w_out, gain,
-    )
-
-
-def place_kernel(arrived_ref, moved_ref):
+        odd, temper, window, dest.reshape(tiles, TILE), window.reshape(tiles, TILE), *tails, near,
+        hidden, far, *projected, w_qkv, w_out, gain,
+    )
+
+
+def place_kernel(odd_ref, arrived_ref, moved_ref, near_ref, far_ref):
     rows = moved_ref.shape[0]
+    rim = near_ref.shape[0]
     devices, padded, channels = arrived_ref.shape
     capacity = padded - 8
     slots = []
@@ -285,55 +331,49 @@
         index = lax.broadcasted_iota(jnp.int32, (chunk, capacity), 0) + start
         hits = jnp.concatenate([one_hot(index == slots[i]) for i in range(devices)], axis=1)
         moved_ref[start : start + chunk] = dot(hits, arrived).astype(jnp.bfloat16)
-
-
-def run_place(arrived, rows):
+    for out_ref, at_end in ((near_ref, 1 - odd_ref[0]), (far_ref, odd_ref[0])):
+        out_ref[...] = moved_ref[pl.ds(pl.multiple_of(at_end * (rows - rim), TILE), rim)]
+
+
+def run_place(odd, arrived, rows):
+    channels = arrived.shape[2]
+    edge = jax.ShapeDtypeStruct((rows // 4, channels), jnp.bfloat16)
     return pl.pallas_call(
         place_kernel,
-        out_shape=jax.ShapeDtypeStruct((rows, arrived.shape[2]), jnp.bfloat16),
-        in_specs=[vmem],
-        out_specs=vmem,
+        out_shape=(jax.ShapeDtypeStruct((rows, channels), jnp.bfloat16), edge, edge),
+        in_specs=[smem, vmem],
+        out_specs=(vmem, vmem, vmem),
         compiler_params=pltpu.CompilerParams(vmem_limit_bytes=vmem_limit),
         cost_estimate=pl.CostEstimate(
             flops=10**9, bytes_accessed=2 * 10**6, transcendentals=0
         ),
         name="place",
-    )(arrived)
-
-
-def exchange(to_right, to_left):
+    )(odd, arrived)
+
+
+def exchange(near, far):
     count = lax.axis_size("wide")
-    forward = [(i, i + 1) for i in range(count - 1)]
-    backward = [(target, source) for source, target in forward]
-    return lax.ppermute(to_right, "wide", forward), lax.ppermute(to_left, "wide", backward)
-
-
-def with_marks(features, windows):
-    channels = features.shape[1]
-    marks = windows + 1
-    digits = jnp.stack([marks // 256, marks % 256], axis=1).reshape(-1)
-    digits = jnp.pad(digits, (0, TAIL * channels - digits.shape[0])).reshape(TAIL, channels)
-    return jnp.concatenate([features, digits.astype(jnp.bfloat16)], axis=0)
+    inner = [(i, i + 1) for i in range(0, count - 1, 2)]
+    outer = [(i, i + 1) for i in range(1, count - 1, 2)]
+    far = lax.ppermute(far, "wide", outer + [(b, a) for a, b in outer])
+    near = lax.ppermute(near, "wide", inner + [(b, a) for a, b in inner])
+    return near, far
 
 
 def body(voxels, regular_window, shifted_window, dest, w_qkv, w_out, gain, temper):
     rows, channels = voxels.shape
-    rim = rows // 4
     devices = lax.axis_size("wide")
-    windows = jnp.stack([regular_window, shifted_window])
-    tails = exchange(
-        with_marks(voxels[rows - rim :], windows[:, rows - rim :]),
-        with_marks(voxels[:rim], windows[:, :rim]),
-    )
+    odd = (lax.axis_index("wide").astype(jnp.int32) % 2).reshape(1)
+    tails = exchange(*run_edges(odd, voxels, regular_window, shifted_window))
     outgoing = run_sublayer(
-        0, devices, temper, regular_window, dest, tails, tails[0], voxels, tails[1], w_qkv, w_out,
-        gain,
+        0, devices, odd, temper, regular_window, dest, tails, tails[0], voxels, tails[1], w_qkv,
+        w_out, gain,
     )
     arrived = lax.all_to_all(outgoing, "wide", split_axis=0, concat_axis=0, tiled=True)
-    moved = run_place(arrived, rows)
-    low, high = exchange(moved[rows - rim :], moved[:rim])
+    moved, near, far = run_place(odd, arrived, rows)
+    near, far = exchange(near, far)
     return run_sublayer(
-        1, 0, temper, shifted_window, dest, tails, low, moved, high, w_qkv, w_out, gain
+        1, 0, odd, temper, shifted_window, dest, tails, near, moved, far, w_qkv, w_out, gain
     )
 
 

time: 82.6 us -> 74.6 us (0.903)
  the two profiles are of different devices: /device:TPU:8 before, /device:TPU:1 now
where the time goes in v3:
time: 74.6 us; the launch traced here: 74.1 us
  blocking collectives  36.2 us (49%)
  Pallas kernels  24.6 us (33%)
  starting transfers between devices  7.39 us (10%)
  waiting for transfers between devices  3.42 us (5%)
  local copies, waits for them, and re-layouts  2.36 us (3%)
    all_to_all x1, blocking collectives, body(): lax.all_to_all(outgoing, 'wide', split_axis=0, concat_axis=0, tiled=True)  36.2 us
    pallas_call x2, Pallas kernels, run_sublayer(): pl.pallas_call(functools.partial(sublayer_kernel, layer, packing), out_sh...  20.3 us
    ppermute x2, starting transfers between devices, exchange(): far = lax.ppermute(far, 'wide', outer + [(b, a) for a, b in outer])  6.89 us
    ppermute x2, waiting for transfers between devices, exchange(): far = lax.ppermute(far, 'wide', outer + [(b, a) for a, b in outer])  3.41 us
    unnamed x20, local copies, waits for them, and re-layouts  2.36 us
    pallas_call x1, Pallas kernels, run_edges(): pl.pallas_call(edges_kernel, out_shape=(shape, shape), in_specs=[smem, vm...  1.86 us
  transfers between devices with their start and end apart: 4, of which 2 were waited for; matrix products, arithmetic and copies ran while one was open for 0% of the time, Pallas kernels for 2%

profile of v3, /device:TPU:1, one launch (start us, length us, event | category | flops | bytes accessed | tf_op | source)
XLA Modules:
  0.0 74.1 jit_solution(2511277012849326254)
XLA Ops:
  0.0 0.0 copy-start.8
  0.0 0.0 copy-start.7
  0.0 1.9 %edges.1 = (bf16[272,256]{1,0:T(8,128)(2,1)}, bf16[272,256]{1,0:T(8,128)(2,1)}) custom-call(s32[1]{0:T(128)} %bitcast.odd_ref, bf16[1024,256]{1,0:T(8,128)(2,1)} %hidden_ref.5, s32[8,128]{1,0:T(8,128)} %bitcast.4, s32[8,128]{1,0:T(8,128)} %bitcast.6), custom_call_target="tpu_custom_call" | custom-call | tf_op jit(solution)/shard_map/edges/pallas_call | solution.py:171
  1.9 0.0 collective-permute-start
  1.9 4.5 %collective-permute-start.1 = (bf16[272,256]{1,0:T(8,128)(2,1)}, bf16[272,256]{1,0:T(8,128)(2,1)S(1)}, u32[]{:S(2)}, u32[]{:S(2)}) collective-permute-start(bf16[272,256]{1,0:T(8,128)(2,1)} %get-tuple-element.17), channel_id=1, source_target_pairs={{1,2},{3,4},{5,6},{7,8},{9,10},{11,12},{13,14},{2,1},{4,3},{6,5},{... | collective-permute-start | bytes 417800 | tf_op jit(solution)/shard_map/ppermute | solution.py:358
  6.4 0.0 copy-start
  6.4 1.0 %copy-done = bf16[1024,256]{1,0:T(8,128)(2,1)S(1)} copy-done((bf16[1024,256]{1,0:T(8,128)(2,1)S(1)}, bf16[1024,256]{1,0:T(8,128)(2,1)}, u32[]{:S(2)}) %copy-start) | copy-done | bytes 524312
  7.5 1.1 %copy-done.4 = bf16[2,256,768]{2,1,0:T(8,128)(2,1)S(1)} copy-done((bf16[2,256,768]{2,1,0:T(8,128)(2,1)S(1)}, bf16[2,256,768]{2,1,0:T(8,128)(2,1)}, u32[]{:S(2)}) %copy-start.4) | copy-done | bytes 786456
  8.6 0.6 project.2
  9.2 0.0 collective-permute-done.near_tail_ref.near_ref
  9.2 0.2 collective-permute-done.1.far_tail_ref.far_ref
  9.4 0.0 copy-done.2
  9.4 0.2 copy-done.6
  9.6 10.2 %sublayer.2 = bf16[16,136,256]{2,1,0:T(8,128)(2,1)S(1)} custom-call(s32[1]{0:T(128)} %bitcast.odd_ref, f32[2,8]{1,0:T(2,128)S(1)} %copy-done.9, s32[1024]{0:T(1024)S(1)} %copy-done.2, s32[8,128]{1,0:T(8,128)S(1)} %bitcast.8, s32[8,128]{1,0:T(8,128)S(1)} %bitcast.5, bf16[272,256]{1,0:T(8,128)(2,1)S(1)} %collective-permute-done.near_tail_ref.near_ref, ...), custom_call_target="tpu_custom_call" | custom-call | flops 8000000000 | bytes 4000000 | tf_op jit(solution)/shard_map/sublayer/pallas_call | solution.py:293
  19.8 36.2 %all_to_all.5.arrived_ref = bf16[16,136,256]{2,1,0:T(8,128)(2,1)S(1)} all-to-all(bf16[16,136,256]{2,1,0:T(8,128)(2,1)S(1)} %sublayer.2), channel_id=1, replica_groups=mesh['parts'=2,'wide'=16] {'wide'}, dimensions={0} | all-to-all | bytes 2228224 | tf_op jit(solution)/shard_map/all_to_all | solution.py:372
  56.0 1.3 %place.1 = (bf16[1024,256]{1,0:T(8,128)(2,1)S(1)}, bf16[256,256]{1,0:T(8,128)(2,1)S(1)}, bf16[256,256]{1,0:T(8,128)(2,1)S(1)}) custom-call(s32[1]{0:T(128)} %bitcast.odd_ref, bf16[16,136,256]{2,1,0:T(8,128)(2,1)S(1)} %all_to_all.5.arrived_ref), custom_call_target="tpu_custom_call" | custom-call | flops 1000000000 | bytes 2000000 | tf_op jit(solution)/shard_map/place/pallas_call | solution.py:341
  57.3 0.0 copy-start.3
  57.3 0.5 collective-permute-start.2
  57.8 2.4 %collective-permute-start.3 = (bf16[256,256]{1,0:T(8,128)(2,1)S(1)}, bf16[256,256]{1,0:T(8,128)(2,1)S(1)}, u32[]{:S(2)}, u32[]{:S(2)}) collective-permute-start(bf16[256,256]{1,0:T(8,128)(2,1)S(1)} %get-tuple-element.23), channel_id=1, source_target_pairs={{1,2},{3,4},{5,6},{7,8},{9,10},{11,12},{13,14},{2,1},{4,3},{6,5},{... | collective-permute-start | bytes 393224 | tf_op jit(solution)/shard_map/ppermute | solution.py:358
  60.2 0.6 project.3
  60.8 0.0 collective-permute-done.2.near_ref
  60.8 3.3 %collective-permute-done.3.far_ref = bf16[256,256]{1,0:T(8,128)(2,1)S(1)} collective-permute-done((bf16[256,256]{1,0:T(8,128)(2,1)S(1)}, bf16[256,256]{1,0:T(8,128)(2,1)S(1)}, u32[]{:S(2)}, u32[]{:S(2)}) %collective-permute-start.3) | collective-permute-done | bytes 131104 | tf_op jit(solution)/shard_map/ppermute | solution.py:358
  64.1 0.0 copy-done.3
  64.1 10.1 %sublayer.3 = bf16[1024,256]{1,0:T(8,128)(2,1)} custom-call(s32[1]{0:T(128)} %bitcast.odd_ref, f32[2,8]{1,0:T(2,128)S(1)} %copy-done.9, s32[1024]{0:T(1024)S(1)} %copy-done.3, s32[8,128]{1,0:T(8,128)S(1)} %bitcast.9, s32[8,128]{1,0:T(8,128)S(1)} %bitcast.7, bf16[272,256]{1,0:T(8,128)(2,1)S(1)} %collective-permute-done.near_tail_ref.near_ref, ...), custom_call_target="tpu_custom_call" | custom-call | flops 8000000000 | bytes 4000000 | tf_op jit(solution)/shard_map/sublayer/pallas_call | solution.py:293
  (11 shorter events, 0.0 us)
Async XLA Ops:
  0.0 9.4 %copy-start.1 = (bf16[1024,256]{1,0:T(8,128)(2,1)S(1)}, bf16[1024,256]{1,0:T(8,128)(2,1)}, u32[]{:S(2)}) copy-start(bf16[1024,256]{1,0:T(8,128)(2,1)} %hidden_ref.5) | copy-start | bytes 1572868
  0.0 9.4 %copy-start.2 = (s32[1024]{0:T(1024)S(1)}, s32[1024]{0:T(1024)}, u32[]{:S(2)}) copy-start(s32[1024]{0:T(1024)} %window_ref.2) | copy-start | bytes 12292
  0.0 9.4 %copy-start.9 = (f32[2,8]{1,0:T(2,128)S(1)}, f32[2,8]{1,0:T(2,128)}, u32[]{:S(2)}) copy-start(f32[2,8]{1,0:T(2,128)} %temper_ref.3) | copy-start | bytes 196
  0.0 9.4 %copy-start.8 = (f32[2,256]{1,0:T(2,128)S(1)}, f32[2,256]{1,0:T(2,128)}, u32[]{:S(2)}) copy-start(f32[2,256]{1,0:T(2,128)} %gain_ref.3) | copy-start | bytes 6148
  0.0 9.4 %copy-start.7 = (s32[1024]{0:T(1024)S(1)}, s32[1024]{0:T(1024)}, u32[]{:S(2)}) copy-start(s32[1024]{0:T(1024)} %param.11) | copy-start | bytes 12292
  1.9 7.3 %collective-permute-start = (bf16[272,256]{1,0:T(8,128)(2,1)}, bf16[272,256]{1,0:T(8,128)(2,1)S(1)}, u32[]{:S(2)}, u32[]{:S(2)}) collective-permute-start(bf16[272,256]{1,0:T(8,128)(2,1)} %get-tuple-element.16), channel_id=1, source_target_pairs={{0,1},{2,3},{4,5},{6,7},{8,9},{10,11},{12,13},{14,15},{1,0},{3,2},... | collective-permute-start | bytes 417800 | tf_op jit(solution)/shard_map/ppermute | solution.py:359
  1.9 7.4 %collective-permute-start.1 = (bf16[272,256]{1,0:T(8,128)(2,1)}, bf16[272,256]{1,0:T(8,128)(2,1)S(1)}, u32[]{:S(2)}, u32[]{:S(2)}) collective-permute-start(bf16[272,256]{1,0:T(8,128)(2,1)} %get-tuple-element.17), channel_id=1, source_target_pairs={{1,2},{3,4},{5,6},{7,8},{9,10},{11,12},{13,14},{2,1},{4,3},{6,5},{... | collective-permute-start | bytes 417800 | tf_op jit(solution)/shard_map/ppermute | solution.py:358
  6.4 1.0 %copy-start = (bf16[1024,256]{1,0:T(8,128)(2,1)S(1)}, bf16[1024,256]{1,0:T(8,128)(2,1)}, u32[]{:S(2)}) copy-start(bf16[1024,256]{1,0:T(8,128)(2,1)} %hidden_ref.5) | copy-start | bytes 1572868
  7.5 1.1 %copy-start.4 = (bf16[2,256,768]{2,1,0:T(8,128)(2,1)S(1)}, bf16[2,256,768]{2,1,0:T(8,128)(2,1)}, u32[]{:S(2)}) copy-start(bf16[2,256,768]{2,1,0:T(8,128)(2,1)} %w_qkv_ref.7) | copy-start | bytes 2359300
  8.6 0.9 %copy-start.6 = (bf16[2,256,256]{2,1,0:T(8,128)(2,1)S(1)}, bf16[2,256,256]{2,1,0:T(8,128)(2,1)}, u32[]{:S(2)}) copy-start(bf16[2,256,256]{2,1,0:T(8,128)(2,1)} %w_out_ref.3) | copy-start | bytes 786436
  56.0 4.2 %copy-start.5 = (bf16[2,256,768]{2,1,0:T(8,128)(2,1)S(1)}, bf16[2,256,768]{2,1,0:T(8,128)(2,1)}, u32[]{:S(2)}) copy-start(bf16[2,256,768]{2,1,0:T(8,128)(2,1)} %w_qkv_ref.7) | copy-start | bytes 2359300
  57.3 6.7 %copy-start.3 = (s32[1024]{0:T(1024)S(1)}, s32[1024]{0:T(1024)}, u32[]{:S(2)}) copy-start(s32[1024]{0:T(1024)} %window_ref.3) | copy-start | bytes 12292
  57.3 3.5 %collective-permute-start.2 = (bf16[256,256]{1,0:T(8,128)(2,1)S(1)}, bf16[256,256]{1,0:T(8,128)(2,1)S(1)}, u32[]{:S(2)}, u32[]{:S(2)}) collective-permute-start(bf16[256,256]{1,0:T(8,128)(2,1)S(1)} %get-tuple-element.21), channel_id=1, source_target_pairs={{0,1},{2,3},{4,5},{6,7},{8,9},{10,11},{12,13},{14,15},{1,0},{3,2},... | collective-permute-start | bytes 393224 | tf_op jit(solution)/shard_map/ppermute | solution.py:359
  57.8 6.3 %collective-permute-start.3 = (bf16[256,256]{1,0:T(8,128)(2,1)S(1)}, bf16[256,256]{1,0:T(8,128)(2,1)S(1)}, u32[]{:S(2)}, u32[]{:S(2)}) collective-permute-start(bf16[256,256]{1,0:T(8,128)(2,1)S(1)} %get-tuple-element.23), channel_id=1, source_target_pairs={{1,2},{3,4},{5,6},{7,8},{9,10},{11,12},{13,14},{2,1},{4,3},{6,5},{... | collective-permute-start | bytes 393224 | tf_op jit(solution)/shard_map/ppermute | solution.py:358
